TPU v7x, 256 devices: a whole 4x4x8 slice. The times are simulated.
256 devices in a mesh: group: 32 (over x, z_hi, core), member: 8 (over z_lo, y).
Axes of the slice: x: 4, y: 4, z: 8 (z_hi: 4, z_lo: 2; z = z_hi * 2 + z_lo), core: 2. Of those that a mesh axis runs over, the one named last changes fastest.
Arguments:
- picture_vectors: bfloat16 [32768, 1152], P(('group', 'member')), may hold values from -1.5 to 1.5
- caption_vectors: bfloat16 [32768, 1152], P(('group', 'member')), may hold values from -1.5 to 1.5
- logit_multiplier: float32 [1], replicated, may hold values from 4 to 16
- logit_offset: float32 [1], replicated, may hold values from -2 to 0
- partner_xor_codes: int32 [4], replicated, may hold values from 1 to 31, as said below
Outputs:
- grad_image: float32 [32768, 1152], P(('group', 'member'))
- text_embedding_gradient: float32 [32768, 1152], P(('group', 'member'))
Inputs may be any that keep to these rules, and one draw needn't show every extreme that they name: `partner_xor_codes`: 4 distinct values; 1 and 31 are always among them.
All inputs are finite; a program needn't handle non-finite values.
Results may differ from a plain program's by a relative error of at most 0.0047.
Values may be sent and summed in bfloat16 or wider, within the bound.
A program may use at most 128 MiB of HBM per device.

v0:
```python
import jax
import jax.numpy as jnp
from jax import lax
from jax.sharding import PartitionSpec as P

EPSILON = 1e-06


def partner(shard, axis, distance):
    return lax.ppermute(shard, axis, [(i, i ^ 1 << distance) for i in range(lax.axis_size(axis))])


def normalized_rows(rows_in):
    values = rows_in.astype(jnp.float32)
    scale = lax.rsqrt(jnp.sum(values * values, axis=-1, keepdims=True) + EPSILON)
    return (values * scale, scale)


def back_unit(unit, scale, grad):
    return (grad - unit * jnp.sum(unit * grad, axis=-1, keepdims=True)) * scale


def tile_coefficients(
    left_operand, right_operand, multiplier_single, offset_amount, main_diagonal_entries
):
    similarity_logits = lax.dot_general(
        left_operand, right_operand, (((1,), (1,)), ((), ())), preferred_element_type=jnp.float32
    )
    multiplier_factor = jax.nn.sigmoid(multiplier_single * similarity_logits + offset_amount)
    if main_diagonal_entries is not None:
        multiplier_factor = multiplier_factor - main_diagonal_entries
    return (multiplier_single * multiplier_factor).astype(jnp.bfloat16)


def bit_count():
    return lax.axis_size("group").bit_length() - 1


def bit_set(round_mask, bit_index):
    return jnp.bitwise_and(jnp.right_shift(round_mask, bit_index), 1) == 1


def fetch_text(payload, round_mask):
    for bit_index in range(bit_count()):
        arrived = partner(payload, "group", bit_index)
        payload = jnp.where(bit_set(round_mask, bit_index), arrived, payload)
    return payload


def send_back(payload, round_mask):
    for bit_index in range(bit_count()):
        arrived = partner(payload, "group", bit_index)
        payload = jnp.where(bit_set(round_mask, bit_index), arrived, payload)
    return payload


def local(picture_vectors, caption_vectors, logit_multiplier, logit_offset, partner_xor_codes):
    unit_u, norm_u = normalized_rows(picture_vectors)
    unit_v, norm_v = normalized_rows(caption_vectors)
    image_b = unit_u.astype(jnp.bfloat16)
    caption_sample_count = unit_v.astype(jnp.bfloat16)
    multiplier_single = logit_multiplier[0]
    offset_amount = logit_offset[0]
    row_count = picture_vectors.shape[0]
    round_total = partner_xor_codes.shape[0]
    member_id = lax.axis_index("member")
    contract_rows = (((0,), (0,)), ((), ()))
    cohort_pictures = lax.all_gather(image_b, "member", axis=0, tiled=True)
    group_count = cohort_pictures.shape[0]
    row_ids = lax.broadcasted_iota(jnp.int32, (group_count, row_count), 0)
    col_ids = lax.broadcasted_iota(jnp.int32, (group_count, row_count), 1)
    main_diagonal_entries = (row_ids == member_id * row_count + col_ids).astype(jnp.float32)
    own_weights = tile_coefficients(
        cohort_pictures,
        caption_sample_count,
        multiplier_single,
        offset_amount,
        main_diagonal_entries,
    )
    image_total = jnp.dot(own_weights, caption_sample_count, preferred_element_type=jnp.float32)
    text_own = lax.dot_general(
        own_weights, cohort_pictures, contract_rows, preferred_element_type=jnp.float32
    )
    for round_id in range(round_total):
        round_mask = partner_xor_codes[round_id]
        counterpart_captions = fetch_text(caption_sample_count, round_mask)
        couple_coefficients = tile_coefficients(
            cohort_pictures, counterpart_captions, multiplier_single, offset_amount, None
        )
        image_total = image_total + jnp.dot(
            couple_coefficients, counterpart_captions, preferred_element_type=jnp.float32
        )
        partner_grad = lax.dot_general(
            couple_coefficients, cohort_pictures, contract_rows, preferred_element_type=jnp.float32
        )
        text_own = text_own + send_back(partner_grad, round_mask)
    image_sum = lax.psum_scatter(image_total, "member", scatter_dimension=0, tiled=True)
    return (back_unit(unit_u, norm_u, image_sum), back_unit(unit_v, norm_v, text_own))


def solution(mesh):
    placed = (P(("group", "member"), None), P(("group", "member"), None), P(), P(), P())
    return jax.shard_map(
        local,
        mesh=mesh,
        in_specs=placed,
        out_specs=(P(("group", "member"), None), P(("group", "member"), None)),
        check_vma=False,
    )
```

profile of v0, /device:TPU:104, one launch (start us, length us, event | category | flops | bytes accessed | tf_op | source)
XLA Modules:
  0.0 489.4 jit_solution(9756889882868573803)
XLA Ops:
  35.2 4.6 collective-permute-start.2
  39.8 31.1 %collective-permute-done.5 = bf16[128,1152]{1,0:T(8,128)(2,1)S(1)} collective-permute-done((bf16[128,1152]{1,0:T(8,128)(2,1)S(1)}, bf16[128,1152]{1,0:T(8,128)(2,1)S(1)}, u32[]{:S(2)}, u32[]{:S(2)}) %collective-permute-start.5) | collective-permute-done | bytes 294944 | tf_op jit(solution)/shard_map/ppermute | solution.py:10
  70.9 6.7 %collective-permute-start.6 = (bf16[128,1152]{1,0:T(8,128)(2,1)S(1)}, bf16[128,1152]{1,0:T(8,128)(2,1)S(1)}, u32[]{:S(2)}, u32[]{:S(2)}) collective-permute-start(bf16[128,1152]{1,0:T(8,128)(2,1)S(1)} %broadcast_select_fusion.21), channel_id=1, source_target_pairs={{0,32},{8,40},{16,48},{24,56},{32,0},{40,8},{48,16},{56,24},{64,96... | collective-permute-start | bytes 884744 | tf_op jit(solution)/shard_map/ppermute | solution.py:10
  77.6 12.7 %collective-permute-start.10 = (bf16[128,1152]{1,0:T(8,128)(2,1)S(1)}, bf16[128,1152]{1,0:T(8,128)(2,1)S(1)}, u32[]{:S(2)}, u32[]{:S(2)}) collective-permute-start(bf16[128,1152]{1,0:T(8,128)(2,1)S(1)} %broadcast_select_fusion.12), channel_id=1, source_target_pairs={{0,32},{8,40},{16,48},{24,56},{32,0},{40,8},{48,16},{56,24},{64,96... | collective-permute-start | bytes 884744 | tf_op jit(solution)/shard_map/ppermute | solution.py:10
  90.4 37.3 %collective-permute-start.14 = (bf16[128,1152]{1,0:T(8,128)(2,1)S(1)}, bf16[128,1152]{1,0:T(8,128)(2,1)S(1)}, u32[]{:S(2)}, u32[]{:S(2)}) collective-permute-start(bf16[128,1152]{1,0:T(8,128)(2,1)S(1)} %broadcast_select_fusion.3), channel_id=1, source_target_pairs={{0,32},{8,40},{16,48},{24,56},{32,0},{40,8},{48,16},{56,24},{64,96... | collective-permute-start | bytes 884744 | tf_op jit(solution)/shard_map/ppermute | solution.py:10
  131.6 9.2 %collective-permute-done.14 = bf16[128,1152]{1,0:T(8,128)(2,1)S(1)} collective-permute-done((bf16[128,1152]{1,0:T(8,128)(2,1)S(1)}, bf16[128,1152]{1,0:T(8,128)(2,1)S(1)}, u32[]{:S(2)}, u32[]{:S(2)}) %collective-permute-start.14) | collective-permute-done | bytes 294944 | tf_op jit(solution)/shard_map/ppermute | solution.py:10
  159.9 5.4 %collective-permute-done.4 = bf16[128,1152]{1,0:T(8,128)(2,1)} collective-permute-done((bf16[128,1152]{1,0:T(8,128)(2,1)S(1)}, bf16[128,1152]{1,0:T(8,128)(2,1)}, u32[]{:S(2)}, u32[]{:S(2)}) %collective-permute-start.4) | collective-permute-done | bytes 294944 | tf_op jit(solution)/shard_map/ppermute | solution.py:10
  203.5 101.0 %collective-permute-done.18 = f32[128,1152]{1,0:T(8,128)S(1)} collective-permute-done((f32[128,1152]{1,0:T(8,128)S(1)}, f32[128,1152]{1,0:T(8,128)S(1)}, u32[]{:S(2)}, u32[]{:S(2)}) %collective-permute-start.18) | collective-permute-done | bytes 589856 | tf_op jit(solution)/shard_map/ppermute | solution.py:10
  304.6 4.5 collective-permute-start.19
  309.1 8.2 %collective-permute-done.23 = f32[128,1152]{1,0:T(8,128)S(1)} collective-permute-done((f32[128,1152]{1,0:T(8,128)S(1)}, f32[128,1152]{1,0:T(8,128)S(1)}, u32[]{:S(2)}, u32[]{:S(2)}) %collective-permute-start.23) | collective-permute-done | bytes 589856 | tf_op jit(solution)/shard_map/ppermute | solution.py:10
  317.3 4.3 collective-permute-start.24
  321.6 8.4 %collective-permute-done.28 = f32[128,1152]{1,0:T(8,128)S(1)} collective-permute-done((f32[128,1152]{1,0:T(8,128)S(1)}, f32[128,1152]{1,0:T(8,128)S(1)}, u32[]{:S(2)}, u32[]{:S(2)}) %collective-permute-start.28) | collective-permute-done | bytes 589856 | tf_op jit(solution)/shard_map/ppermute | solution.py:10
  330.1 4.3 collective-permute-start.29
  334.4 8.3 %collective-permute-done.33 = f32[128,1152]{1,0:T(8,128)S(1)} collective-permute-done((f32[128,1152]{1,0:T(8,128)S(1)}, f32[128,1152]{1,0:T(8,128)S(1)}, u32[]{:S(2)}, u32[]{:S(2)}) %collective-permute-start.33) | collective-permute-done | bytes 589856 | tf_op jit(solution)/shard_map/ppermute | solution.py:10
  342.8 4.3 collective-permute-start.34
  347.1 23.1 %collective-permute-done.19 = f32[128,1152]{1,0:T(8,128)S(1)} collective-permute-done((f32[128,1152]{1,0:T(8,128)S(1)}, f32[128,1152]{1,0:T(8,128)S(1)}, u32[]{:S(2)}, u32[]{:S(2)}) %collective-permute-start.19) | collective-permute-done | bytes 589856 | tf_op jit(solution)/shard_map/ppermute | solution.py:10
  370.6 17.5 %collective-permute-done.24 = f32[128,1152]{1,0:T(8,128)S(1)} collective-permute-done((f32[128,1152]{1,0:T(8,128)S(1)}, f32[128,1152]{1,0:T(8,128)S(1)}, u32[]{:S(2)}, u32[]{:S(2)}) %collective-permute-start.24) | collective-permute-done | bytes 589856 | tf_op jit(solution)/shard_map/ppermute | solution.py:10
  388.5 12.3 %collective-permute-done.29 = f32[128,1152]{1,0:T(8,128)S(1)} collective-permute-done((f32[128,1152]{1,0:T(8,128)S(1)}, f32[128,1152]{1,0:T(8,128)S(1)}, u32[]{:S(2)}, u32[]{:S(2)}) %collective-permute-start.29) | collective-permute-done | bytes 589856 | tf_op jit(solution)/shard_map/ppermute | solution.py:10
  401.2 11.5 %collective-permute-done.34 = f32[128,1152]{1,0:T(8,128)S(1)} collective-permute-done((f32[128,1152]{1,0:T(8,128)S(1)}, f32[128,1152]{1,0:T(8,128)S(1)}, u32[]{:S(2)}, u32[]{:S(2)}) %collective-permute-start.34) | collective-permute-done | bytes 589856 | tf_op jit(solution)/shard_map/ppermute | solution.py:10
  418.9 10.2 %collective-permute-done.35 = f32[128,1152]{1,0:T(8,128)S(1)} collective-permute-done((f32[128,1152]{1,0:T(8,128)S(1)}, f32[128,1152]{1,0:T(8,128)S(1)}, u32[]{:S(2)}, u32[]{:S(2)}) %collective-permute-start.35) | collective-permute-done | bytes 589856 | tf_op jit(solution)/shard_map/ppermute | solution.py:10
  430.5 11.2 %collective-permute-done.21 = f32[128,1152]{1,0:T(8,128)S(1)} collective-permute-done((f32[128,1152]{1,0:T(8,128)S(1)}, f32[128,1152]{1,0:T(8,128)S(1)}, u32[]{:S(2)}, u32[]{:S(2)}) %collective-permute-start.21) | collective-permute-done | bytes 589856 | tf_op jit(solution)/shard_map/ppermute | solution.py:10
  441.7 12.6 %collective-permute-done.26 = f32[128,1152]{1,0:T(8,128)S(1)} collective-permute-done((f32[128,1152]{1,0:T(8,128)S(1)}, f32[128,1152]{1,0:T(8,128)S(1)}, u32[]{:S(2)}, u32[]{:S(2)}) %collective-permute-start.26) | collective-permute-done | bytes 589856 | tf_op jit(solution)/shard_map/ppermute | solution.py:10
  454.4 12.6 %collective-permute-done.31 = f32[128,1152]{1,0:T(8,128)S(1)} collective-permute-done((f32[128,1152]{1,0:T(8,128)S(1)}, f32[128,1152]{1,0:T(8,128)S(1)}, u32[]{:S(2)}, u32[]{:S(2)}) %collective-permute-start.31) | collective-permute-done | bytes 589856 | tf_op jit(solution)/shard_map/ppermute | solution.py:10
  467.0 10.8 %collective-permute-done.36 = f32[128,1152]{1,0:T(8,128)S(1)} collective-permute-done((f32[128,1152]{1,0:T(8,128)S(1)}, f32[128,1152]{1,0:T(8,128)S(1)}, u32[]{:S(2)}, u32[]{:S(2)}) %collective-permute-start.36) | collective-permute-done | bytes 589856 | tf_op jit(solution)/shard_map/ppermute | solution.py:10
  (134 shorter events, 88.7 us)
Async XLA Ops:
  7.2 158.2 %all-gather.2.cloned.1.call-start = ((), (), s32[]{:S(2)}) async-start(), calls=%async_computation.1 | async-start | bytes 2654208 | tf_op jit(solution)/shard_map/all_gather | solution.py:68
  17.5 461.6 %reduce-scatter.2.cloned.1.call-start = ((), (), s32[]{:S(2)}) async-start(), calls=%async_computation.2 | async-start | bytes 5308416 | tf_op jit(solution)/shard_map/reduce_scatter | solution.py:97
  29.2 41.6 %collective-permute-start.5 = (bf16[128,1152]{1,0:T(8,128)(2,1)S(1)}, bf16[128,1152]{1,0:T(8,128)(2,1)S(1)}, u32[]{:S(2)}, u32[]{:S(2)}) collective-permute-start(bf16[128,1152]{1,0:T(8,128)(2,1)S(1)} %get-tuple-element.4), channel_id=1, source_target_pairs={{0,16},{8,24},{16,0},{24,8},{32,48},{40,56},{48,32},{56,40},{64,80... | collective-permute-start | bytes 884744 | tf_op jit(solution)/shard_map/ppermute | solution.py:10
  32.2 45.4 %collective-permute-start.9 = (bf16[128,1152]{1,0:T(8,128)(2,1)S(1)}, bf16[128,1152]{1,0:T(8,128)(2,1)S(1)}, u32[]{:S(2)}, u32[]{:S(2)}) collective-permute-start(bf16[128,1152]{1,0:T(8,128)(2,1)S(1)} %get-tuple-element.6), channel_id=1, source_target_pairs={{0,16},{8,24},{16,0},{24,8},{32,48},{40,56},{48,32},{56,40},{64,80... | collective-permute-start | bytes 884744 | tf_op jit(solution)/shard_map/ppermute | solution.py:10
  32.3 58.0 %collective-permute-start.13 = (bf16[128,1152]{1,0:T(8,128)(2,1)S(1)}, bf16[128,1152]{1,0:T(8,128)(2,1)S(1)}, u32[]{:S(2)}, u32[]{:S(2)}) collective-permute-start(bf16[128,1152]{1,0:T(8,128)(2,1)S(1)} %get-tuple-element.5), channel_id=1, source_target_pairs={{0,16},{8,24},{16,0},{24,8},{32,48},{40,56},{48,32},{56,40},{64,80... | collective-permute-start | bytes 884744 | tf_op jit(solution)/shard_map/ppermute | solution.py:10
  35.2 92.5 %collective-permute-start.2 = (bf16[128,1152]{1,0:T(8,128)(2,1)S(1)}, bf16[128,1152]{1,0:T(8,128)(2,1)S(1)}, u32[]{:S(2)}, u32[]{:S(2)}) collective-permute-start(bf16[128,1152]{1,0:T(8,128)(2,1)S(1)} %broadcast_select_fusion.30), channel_id=1, source_target_pairs={{0,32},{8,40},{16,48},{24,56},{32,0},{40,8},{48,16},{56,24},{64,96... | collective-permute-start | bytes 884744 | tf_op jit(solution)/shard_map/ppermute | solution.py:10
  70.9 58.5 %collective-permute-start.6 = (bf16[128,1152]{1,0:T(8,128)(2,1)S(1)}, bf16[128,1152]{1,0:T(8,128)(2,1)S(1)}, u32[]{:S(2)}, u32[]{:S(2)}) collective-permute-start(bf16[128,1152]{1,0:T(8,128)(2,1)S(1)} %broadcast_select_fusion.21), channel_id=1, source_target_pairs={{0,32},{8,40},{16,48},{24,56},{32,0},{40,8},{48,16},{56,24},{64,96... | collective-permute-start | bytes 884744 | tf_op jit(solution)/shard_map/ppermute | solution.py:10
  77.6 52.4 %collective-permute-start.10 = (bf16[128,1152]{1,0:T(8,128)(2,1)S(1)}, bf16[128,1152]{1,0:T(8,128)(2,1)S(1)}, u32[]{:S(2)}, u32[]{:S(2)}) collective-permute-start(bf16[128,1152]{1,0:T(8,128)(2,1)S(1)} %broadcast_select_fusion.12), channel_id=1, source_target_pairs={{0,32},{8,40},{16,48},{24,56},{32,0},{40,8},{48,16},{56,24},{64,96... | collective-permute-start | bytes 884744 | tf_op jit(solution)/shard_map/ppermute | solution.py:10
  90.4 50.4 %collective-permute-start.14 = (bf16[128,1152]{1,0:T(8,128)(2,1)S(1)}, bf16[128,1152]{1,0:T(8,128)(2,1)S(1)}, u32[]{:S(2)}, u32[]{:S(2)}) collective-permute-start(bf16[128,1152]{1,0:T(8,128)(2,1)S(1)} %broadcast_select_fusion.3), channel_id=1, source_target_pairs={{0,32},{8,40},{16,48},{24,56},{32,0},{40,8},{48,16},{56,24},{64,96... | collective-permute-start | bytes 884744 | tf_op jit(solution)/shard_map/ppermute | solution.py:10
  150.5 27.5 %collective-permute-start.12 = (bf16[128,1152]{1,0:T(8,128)(2,1)S(1)}, bf16[128,1152]{1,0:T(8,128)(2,1)}, u32[]{:S(2)}, u32[]{:S(2)}) collective-permute-start(bf16[128,1152]{1,0:T(8,128)(2,1)S(1)} %broadcast_select_fusion.16), channel_id=1, source_target_pairs={{0,128},{8,136},{16,144},{24,152},{32,160},{40,168},{48,176},{56,1... | collective-permute-start | bytes 884744 | tf_op jit(solution)/shard_map/ppermute | solution.py:10
  195.0 109.5 %collective-permute-start.18 = (f32[128,1152]{1,0:T(8,128)S(1)}, f32[128,1152]{1,0:T(8,128)S(1)}, u32[]{:S(2)}, u32[]{:S(2)}) collective-permute-start(f32[128,1152]{1,0:T(8,128)S(1)} %broadcast_select_fusion.27), channel_id=1, source_target_pairs={{0,16},{8,24},{16,0},{24,8},{32,48},{40,56},{48,32},{56,40},{64,80... | collective-permute-start | bytes 1769480 | tf_op jit(solution)/shard_map/ppermute | solution.py:10
  196.2 121.1 %collective-permute-start.23 = (f32[128,1152]{1,0:T(8,128)S(1)}, f32[128,1152]{1,0:T(8,128)S(1)}, u32[]{:S(2)}, u32[]{:S(2)}) collective-permute-start(f32[128,1152]{1,0:T(8,128)S(1)} %broadcast_select_fusion.18), channel_id=1, source_target_pairs={{0,16},{8,24},{16,0},{24,8},{32,48},{40,56},{48,32},{56,40},{64,80... | collective-permute-start | bytes 1769480 | tf_op jit(solution)/shard_map/ppermute | solution.py:10
  200.3 129.7 %collective-permute-start.28 = (f32[128,1152]{1,0:T(8,128)S(1)}, f32[128,1152]{1,0:T(8,128)S(1)}, u32[]{:S(2)}, u32[]{:S(2)}) collective-permute-start(f32[128,1152]{1,0:T(8,128)S(1)} %broadcast_select_fusion.9), channel_id=1, source_target_pairs={{0,16},{8,24},{16,0},{24,8},{32,48},{40,56},{48,32},{56,40},{64,80... | collective-permute-start | bytes 1769480 | tf_op jit(solution)/shard_map/ppermute | solution.py:10
  200.5 142.2 %collective-permute-start.33 = (f32[128,1152]{1,0:T(8,128)S(1)}, f32[128,1152]{1,0:T(8,128)S(1)}, u32[]{:S(2)}, u32[]{:S(2)}) collective-permute-start(f32[128,1152]{1,0:T(8,128)S(1)} %broadcast_select_fusion), channel_id=1, source_target_pairs={{0,16},{8,24},{16,0},{24,8},{32,48},{40,56},{48,32},{56,40},{64,80... | collective-permute-start | bytes 1769480 | tf_op jit(solution)/shard_map/ppermute | solution.py:10
  304.6 65.6 %collective-permute-start.19 = (f32[128,1152]{1,0:T(8,128)S(1)}, f32[128,1152]{1,0:T(8,128)S(1)}, u32[]{:S(2)}, u32[]{:S(2)}) collective-permute-start(f32[128,1152]{1,0:T(8,128)S(1)} %broadcast_select_fusion.29), channel_id=1, source_target_pairs={{0,32},{8,40},{16,48},{24,56},{32,0},{40,8},{48,16},{56,24},{64,96... | collective-permute-start | bytes 1769480 | tf_op jit(solution)/shard_map/ppermute | solution.py:10
  317.3 70.8 %collective-permute-start.24 = (f32[128,1152]{1,0:T(8,128)S(1)}, f32[128,1152]{1,0:T(8,128)S(1)}, u32[]{:S(2)}, u32[]{:S(2)}) collective-permute-start(f32[128,1152]{1,0:T(8,128)S(1)} %broadcast_select_fusion.20), channel_id=1, source_target_pairs={{0,32},{8,40},{16,48},{24,56},{32,0},{40,8},{48,16},{56,24},{64,96... | collective-permute-start | bytes 1769480 | tf_op jit(solution)/shard_map/ppermute | solution.py:10
  330.1 70.7 %collective-permute-start.29 = (f32[128,1152]{1,0:T(8,128)S(1)}, f32[128,1152]{1,0:T(8,128)S(1)}, u32[]{:S(2)}, u32[]{:S(2)}) collective-permute-start(f32[128,1152]{1,0:T(8,128)S(1)} %broadcast_select_fusion.11), channel_id=1, source_target_pairs={{0,32},{8,40},{16,48},{24,56},{32,0},{40,8},{48,16},{56,24},{64,96... | collective-permute-start | bytes 1769480 | tf_op jit(solution)/shard_map/ppermute | solution.py:10
  342.8 69.9 %collective-permute-start.34 = (f32[128,1152]{1,0:T(8,128)S(1)}, f32[128,1152]{1,0:T(8,128)S(1)}, u32[]{:S(2)}, u32[]{:S(2)}) collective-permute-start(f32[128,1152]{1,0:T(8,128)S(1)} %broadcast_select_fusion.2), channel_id=1, source_target_pairs={{0,32},{8,40},{16,48},{24,56},{32,0},{40,8},{48,16},{56,24},{64,96... | collective-permute-start | bytes 1769480 | tf_op jit(solution)/shard_map/ppermute | solution.py:10
  370.3 42.7 %collective-permute-start.20 = (f32[128,1152]{1,0:T(8,128)S(1)}, f32[128,1152]{1,0:T(8,128)S(1)}, u32[]{:S(2)}, u32[]{:S(2)}) collective-permute-start(f32[128,1152]{1,0:T(8,128)S(1)} %broadcast_select_fusion.31), channel_id=1, source_target_pairs={{0,64},{8,72},{16,80},{24,88},{32,96},{40,104},{48,112},{56,120},{... | collective-permute-start | bytes 1769480 | tf_op jit(solution)/shard_map/ppermute | solution.py:10
  388.2 26.8 %collective-permute-start.25 = (f32[128,1152]{1,0:T(8,128)S(1)}, f32[128,1152]{1,0:T(8,128)S(1)}, u32[]{:S(2)}, u32[]{:S(2)}) collective-permute-start(f32[128,1152]{1,0:T(8,128)S(1)} %broadcast_select_fusion.22), channel_id=1, source_target_pairs={{0,64},{8,72},{16,80},{24,88},{32,96},{40,104},{48,112},{56,120},{... | collective-permute-start | bytes 1769480 | tf_op jit(solution)/shard_map/ppermute | solution.py:10
  413.1 28.6 %collective-permute-start.21 = (f32[128,1152]{1,0:T(8,128)S(1)}, f32[128,1152]{1,0:T(8,128)S(1)}, u32[]{:S(2)}, u32[]{:S(2)}) collective-permute-start(f32[128,1152]{1,0:T(8,128)S(1)} %broadcast_select_fusion.33), channel_id=1, source_target_pairs={{0,128},{8,136},{16,144},{24,152},{32,160},{40,168},{48,176},{56,1... | collective-permute-start | bytes 1769480 | tf_op jit(solution)/shard_map/ppermute | solution.py:10
  415.1 39.3 %collective-permute-start.26 = (f32[128,1152]{1,0:T(8,128)S(1)}, f32[128,1152]{1,0:T(8,128)S(1)}, u32[]{:S(2)}, u32[]{:S(2)}) collective-permute-start(f32[128,1152]{1,0:T(8,128)S(1)} %broadcast_select_fusion.24), channel_id=1, source_target_pairs={{0,128},{8,136},{16,144},{24,152},{32,160},{40,168},{48,176},{56,1... | collective-permute-start | bytes 1769480 | tf_op jit(solution)/shard_map/ppermute | solution.py:10
  416.9 50.1 %collective-permute-start.31 = (f32[128,1152]{1,0:T(8,128)S(1)}, f32[128,1152]{1,0:T(8,128)S(1)}, u32[]{:S(2)}, u32[]{:S(2)}) collective-permute-start(f32[128,1152]{1,0:T(8,128)S(1)} %broadcast_select_fusion.15), channel_id=1, source_target_pairs={{0,128},{8,136},{16,144},{24,152},{32,160},{40,168},{48,176},{56,1... | collective-permute-start | bytes 1769480 | tf_op jit(solution)/shard_map/ppermute | solution.py:10
  429.1 48.7 %collective-permute-start.36 = (f32[128,1152]{1,0:T(8,128)S(1)}, f32[128,1152]{1,0:T(8,128)S(1)}, u32[]{:S(2)}, u32[]{:S(2)}) collective-permute-start(f32[128,1152]{1,0:T(8,128)S(1)} %broadcast_select_fusion.6), channel_id=1, source_target_pairs={{0,128},{8,136},{16,144},{24,152},{32,160},{40,168},{48,176},{56,1... | collective-permute-start | bytes 1769480 | tf_op jit(solution)/shard_map/ppermute | solution.py:10
  (26 other events, 425.2 us)
Sparse Core Ops, SparseCore 0:
  17.7 73.9 all-gather.1
  193.9 171.1 reduce-scatter.1
where the time goes:
time: 490 us; the launch traced here: 489 us
  waiting for transfers between devices  307 us (63%)
  starting transfers between devices  115 us (23%)
  between operations  28.6 us (6%)
  matrix products  20.1 us (4%)
  other arithmetic  15.5 us (3%)
    ppermute x37, waiting for transfers between devices, partner(): lax.ppermute(shard, axis, [(i, i ^ 1 << distance) for i in range(lax.axis...  307 us
    ppermute x37, starting transfers between devices, partner(): lax.ppermute(shard, axis, [(i, i ^ 1 << distance) for i in range(lax.axis...  115 us
  transfers between devices with their start and end apart: 39, of which 21 were waited for; matrix products, arithmetic and copies ran while one was open for 6% of the time, Pallas kernels for 0%

commit v1 on v0

v1 whole, which is shorter than its diff:
```python
import jax
import jax.numpy as jnp
from jax import lax
from jax.experimental import pallas as pl
from jax.experimental.pallas import tpu as pltpu
from jax.sharding import PartitionSpec as P

EPSILON = 1e-06
MESH = pl.DeviceIdType.MESH
BF = jnp.bfloat16
F32 = jnp.float32
WHOLE = (("group", "member"), None)
PARTS = 4
OWN, LO, Y1, Y3, LO_Y1, LO_Y3, Y2, LO_Y2 = range(8)


def flip(value, code):
    if code == 0:
        return value
    if code == 1:
        return value + 1 - 2 * (value % 2)
    if code == 2:
        return (value + 2) % 4
    return 3 - value


def peer(x=0, z=0, core=0, lo=0, y=0):
    group, member = lax.axis_index("group"), lax.axis_index("member")
    at_x, at_z, at_core = group // 8, (group // 2) % 4, group % 2
    at_lo, at_y = member // 4, member % 4
    return (
        flip(at_x, x) * 8 + flip(at_z, z) * 2 + flip(at_core, core),
        flip(at_lo, lo) * 4 + flip(at_y, y),
    )


PEERS = (
    dict(core=1),
    dict(x=1),
    dict(x=3),
    dict(x=3, core=1),
    dict(z=1),
    dict(z=3),
    dict(lo=1),
    dict(y=1),
    dict(y=3),
)


def unit_rows(raw):
    values = raw.astype(F32)
    scale = lax.rsqrt(jnp.sum(values * values, axis=-1, keepdims=True) + EPSILON)
    return values * scale, scale


def back_unit(unit, scale, grad):
    return (grad - unit * jnp.sum(unit * grad, axis=-1, keepdims=True)) * scale


def choose(code, zero, one, two, three):
    low = jnp.where(code == 1, one, zero)
    high = jnp.where(code == 3, three, two)
    return jnp.where(code >= 2, high, low)


def scratch(rows, wide):
    piece = rows // PARTS
    half = piece // 2
    unit = pltpu.VMEM((rows, wide), BF)
    both = pltpu.VMEM((2 * half, wide), BF)
    pair = pltpu.VMEM((2 * piece, wide), BF)
    each = lambda ref: [ref] * PARTS
    return dict(
        img=pltpu.VMEM((8 * rows, wide), BF),
        txt=pltpu.VMEM((5 * rows, wide), BF),
        wgt=pltpu.VMEM((5 * rows, 8 * rows), BF),
        bank=each(pltpu.VMEM((8, piece, wide), BF)),
        g_near=each(both),
        g_far=each(both),
        g_s3=each(both),
        g_s21=each(both),
        g_s23=each(both),
        g_r11=each(both),
        g_r13=each(both),
        g_r21=each(both),
        g_r23=each(both),
        d_own=each(pair),
        d_core=each(pair),
        b_near=each(both),
        b_far=each(both),
        b_s3=each(both),
        b_s21=each(both),
        b_s23=each(both),
        b_r11=each(both),
        b_r13=each(both),
        b_r21=each(both),
        b_r23=each(both),
        d31_out=each(pltpu.VMEM((piece, wide), BF)),
        d31_in=each(pltpu.VMEM((piece, wide), BF)),
        z_sum=each(pltpu.VMEM((4, piece, wide), F32)),
        z_s=each(pltpu.VMEM((3, piece, wide), BF)),
        z_r2=each(pltpu.VMEM((piece, wide), BF)),
        z_r1=each(pltpu.VMEM((piece, wide), BF)),
        z_r3=each(pltpu.VMEM((piece, wide), BF)),
        d_text=pltpu.VMEM((2 * rows, wide), F32),
        d_text_in=pltpu.VMEM((rows, wide), F32),
        d_img=pltpu.VMEM((8 * rows, wide), F32),
        i_s=[unit] * 7,
        i_r=[unit] * 7,
        scale_u=pltpu.VMEM((rows, 1), F32),
        scale_v=pltpu.VMEM((rows, 1), F32),
        send=pltpu.SemaphoreType.DMA((160,)),
        recv=pltpu.SemaphoreType.DMA((160,)),
    )


def kernel(pic_ref, cap_ref, mult_ref, off_ref, code_ref, gi_ref, gt_ref, s):
    rows, wide = pic_ref.shape
    piece = rows // PARTS
    half = piece // 2
    img, txt, wgt = s["img"], s["txt"], s["wgt"]
    copies = {}

    def send(name, src, dst, **to):
        at = len(copies)
        copy = pltpu.make_async_remote_copy(
            src_ref=src,
            dst_ref=dst,
            send_sem=s["send"].at[at],
            recv_sem=s["recv"].at[at],
            device_id=peer(**to),
            device_id_type=MESH,
        )
        copies[name] = copy
        copy.start()

    def arrived(*names):
        for name in names:
            copies[name].wait_recv()

    def slot(at):
        return pl.ds(at * rows, rows)

    def part(j):
        return pl.ds(j * piece, piece)

    barrier = pltpu.get_barrier_semaphore()
    for to in PEERS:
        pl.semaphore_signal(barrier, inc=1, device_id=peer(**to), device_id_type=MESH)

    mult, off = mult_ref[0], off_ref[0]
    codes = [code_ref[i] for i in range(4)]
    code_a, code_b = jnp.int32(99), jnp.int32(-1)
    for code in codes:
        code_a = jnp.minimum(code_a, jnp.where(code == 1, 99, code))
        code_b = jnp.maximum(code_b, jnp.where(code == 31, -1, code))
    core_of = [code_a & 1, code_b & 1]
    z_of = [(code_a >> 1) & 3, (code_b >> 1) & 3]
    x_of = [(code_a >> 3) & 3, (code_b >> 3) & 3]

    unit_v, scale_v = unit_rows(cap_ref[...])
    s["scale_v"][...] = scale_v
    own_text = unit_v.astype(BF)
    txt[slot(0), :] = own_text
    for j in range(PARTS):
        s["bank"][j][0] = own_text[j * piece : (j + 1) * piece]
    unit_u, scale_u = unit_rows(pic_ref[...])
    s["scale_u"][...] = scale_u
    img[slot(OWN), :] = unit_u.astype(BF)
    pl.semaphore_wait(barrier, len(PEERS))

    def z_first(j):
        src = s["bank"][j].at[0]
        send(f"z1_{j}", src, s["bank"][j].at[1], z=1)
        send(f"z3_{j}", src, s["bank"][j].at[3], z=3)

    def z_second(j):
        bank = s["bank"][j]
        near, far = pl.ds(0, half), pl.ds(half, half)
        arrived(f"z1_{j}")
        send(f"z2a_{j}", bank.at[1, near], bank.at[2, near], z=3)
        arrived(f"z3_{j}")
        send(f"z2b_{j}", bank.at[3, far], bank.at[2, far], z=1)
        send(f"t31_{j}", bank.at[3], txt.at[pl.ds(2 * rows + j * piece, piece)], x=3, core=1)
        send(f"c1_{j}", bank.at[1], bank.at[5], core=1)
        send(f"c3_{j}", bank.at[3], bank.at[7], core=1)

    def z_done(j):
        bank = s["bank"][j]
        arrived(f"z2a_{j}", f"z2b_{j}")
        send(f"c2_{j}", bank.at[2], bank.at[6], core=1)

    def x_send(tag, j, far, where):
        near_ref, far_ref, s3 = s[tag + "near"][j], s[tag + "far"][j], s[tag + "s3"][j]
        send(f"{tag}11_{j}", near_ref, s[tag + "r11"][j], x=1)
        for m in range(2):
            at = pl.ds(m * half, half)
            s3[at, :] = jnp.where(x_of[m] == 2, far_ref[at, :], near_ref[at, :])
        send(f"{tag}13_{j}", s3, s[tag + "r13"][j], x=3)

    def x_second(tag, j):
        far_ref = s[tag + "far"][j]
        for side, name in ((3, "11"), (1, "13")):
            arrived(f"{tag}{name}_{j}")
            got, out = s[f"{tag}r{name}"][j], s[f"{tag}s2{side}"][j]
            for m in range(2):
                at = pl.ds(m * half, half)
                out[at, :] = jnp.where(x_of[m] == 2, got[at, :], far_ref[at, :])
            send(f"{tag}2{side}_{j}", out, s[f"{tag}r2{side}"][j], x=side)

    def x_done(tag, j, m):
        at = pl.ds(m * half, half)
        r11, r13, r21, r23 = (s[f"{tag}r{n}"][j][at, :] for n in ("11", "13", "21", "23"))
        near = choose(x_of[m], s[tag + "near"][j][at, :], r11, r23, r13)
        far = choose(x_of[m], s[tag + "far"][j][at, :], r21, r21, r23)
        return near, far

    def x_text(j):
        bank = s["bank"][j]
        arrived(f"c1_{j}", f"c2_{j}", f"c3_{j}")
        for m in range(2):
            at = pl.ds(m * half, half)
            picked = bank[core_of[m] * 4 + z_of[m]]
            s["g_near"][j][at, :] = picked[:half]
            s["g_far"][j][at, :] = picked[half:]
        x_send("g_", j, None, None)

    def text_in(j):
        arrived(f"g_21_{j}", f"g_23_{j}")
        for m in range(2):
            near, far = x_done("g_", j, m)
            base = 3 * rows + (2 * j + m) * piece
            txt[pl.ds(base, half), :] = near
            txt[pl.ds(base + half, half), :] = far

    def weigh(start, count, positive):
        def tile(i, carry):
            cols = pl.ds(pl.multiple_of(i * 2 * rows, 2 * rows), 2 * rows)
            logits = lax.dot_general(
                txt[pl.ds(start, count), :],
                img[cols, :],
                (((1,), (1,)), ((), ())),
                preferred_element_type=F32,
            )
            factor = jax.nn.sigmoid(mult * logits + off)
            if positive:
                row = lax.broadcasted_iota(jnp.int32, factor.shape, 0)
                col = lax.broadcasted_iota(jnp.int32, factor.shape, 1) + i * 2 * rows
                factor = factor - jnp.where((row == col) & (row < rows), 1.0, 0.0)
            wgt[pl.ds(start, count), cols] = (mult * factor).astype(BF)
            return carry

        lax.fori_loop(0, 4, tile, 0)

    def text_grad(start, count):
        return jnp.dot(wgt[pl.ds(start, count), :], img[...], preferred_element_type=F32)

    def image_grad(start, count, at):
        cols = pl.ds(at * rows, 2 * rows)
        return lax.dot_general(
            wgt[pl.ds(start, count), cols],
            txt[pl.ds(start, count), :],
            (((0,), (0,)), ((), ())),
            preferred_element_type=F32,
        )

    def grads_out(j):
        start = 3 * rows + 2 * j * piece
        weigh(start, 2 * piece, False)
        s["d_own"][j][...] = text_grad(start, 2 * piece).astype(BF)
        send(f"dc_{j}", s["d_own"][j], s["d_core"][j], core=1)

    def grads_x(j):
        arrived(f"dc_{j}")
        own, other = s["d_own"][j], s["d_core"][j]
        for m in range(2):
            at = pl.ds(m * half, half)
            for name, base in (("near", m * piece), ("far", m * piece + half)):
                take = pl.ds(base, half)
                s["b_" + name][j][at, :] = jnp.where(core_of[m] == 1, other[take, :], own[take, :])
        x_send("b_", j, None, None)

    def grads_z(j):
        arrived(f"b_21_{j}", f"b_23_{j}", f"d31_{j}")
        total = s["z_sum"][j]
        zero = jnp.zeros((half, wide), F32)
        got = [x_done("b_", j, m) for m in range(2)]
        for h in range(2):
            at = pl.ds(h * half, half)
            a, b = got[0][h].astype(F32), got[1][h].astype(F32)
            for k in range(4):
                value = jnp.where(z_of[0] == k, a, zero) + jnp.where(z_of[1] == k, b, zero)
                if k == 3:
                    value = value + s["d31_in"][j][at, :].astype(F32)
                total[k, at, :] = value
        out = s["z_s"][j]
        out[0] = total[2].astype(BF)
        near, far = pl.ds(0, half), pl.ds(half, half)
        send(f"dz2a_{j}", out.at[0, near], s["z_r2"][j].at[near], z=3)
        send(f"dz2b_{j}", out.at[0, far], s["z_r2"][j].at[far], z=1)

    def grads_z_second(j):
        total, out, got = s["z_sum"][j], s["z_s"][j], s["z_r2"][j]
        near, far = pl.ds(0, half), pl.ds(half, half)
        arrived(f"dz2a_{j}")
        out[1, far, :] = total[1, far, :].astype(BF)
        out[1, near, :] = (total[1, near, :] + got[near, :].astype(F32)).astype(BF)
        send(f"dz1_{j}", out.at[1], s["z_r1"][j], z=1)
        arrived(f"dz2b_{j}")
        out[2, near, :] = total[3, near, :].astype(BF)
        out[2, far, :] = (total[3, far, :] + got[far, :].astype(F32)).astype(BF)
        send(f"dz3_{j}", out.at[2], s["z_r3"][j], z=3)

    def text_out(j):
        arrived(f"dz1_{j}", f"dz3_{j}")
        total = s["z_sum"][j][0] + s["z_r1"][j][...].astype(F32) + s["z_r3"][j][...].astype(F32)
        total = total + s["d_text"][part(j), :] + s["d_text_in"][part(j), :]
        scale = s["scale_v"][part(j), :]
        unit = cap_ref[part(j), :].astype(F32) * scale
        gt_ref[part(j), :] = back_unit(unit, scale, total)

    def early():
        weigh(0, 2 * rows, True)
        s["d_text"][...] = text_grad(0, 2 * rows)
        send("d1", s["d_text"].at[slot(1)], s["d_text_in"], core=1)

    def early31():
        weigh(2 * rows, rows, False)
        grad = text_grad(2 * rows, rows).astype(BF)
        for j in range(PARTS):
            s["d31_out"][j][...] = grad[j * piece : (j + 1) * piece]
            send(f"d31_{j}", s["d31_out"][j], s["d31_in"][j], x=3, core=1)

    def early_image():
        def tile(i, carry):
            at = pl.ds(pl.multiple_of(i * 2 * rows, 2 * rows), 2 * rows)
            s["d_img"][at, :] = lax.dot_general(
                wgt[pl.ds(0, 3 * rows), at],
                txt[pl.ds(0, 3 * rows), :],
                (((0,), (0,)), ((), ())),
                preferred_element_type=F32,
            )
            return carry

        lax.fori_loop(0, 4, tile, 0)

    def late_image(at):
        here = pl.ds(at * rows, 2 * rows)
        s["d_img"][here, :] = s["d_img"][here, :] + image_grad(3 * rows, 2 * rows, at)

    def image_send(name, n, value, **to):
        s["i_s"][n][...] = value.astype(BF)
        send(name, s["i_s"][n], s["i_r"][n], **to)

    def grad_of(at):
        return s["d_img"][slot(at), :]

    def got(n):
        return s["i_r"][n][...].astype(F32)

    def image_first():
        late_image(Y2)
        image_send("u7", 0, grad_of(LO_Y2), y=1)
        image_send("u6", 1, grad_of(Y2), y=3)
        late_image(LO_Y1)
        image_send("u4", 2, grad_of(LO_Y1), y=1)
        late_image(Y1)
        image_send("u3", 3, grad_of(Y3), y=3)
        late_image(OWN)

    def image_second():
        arrived("u7")
        image_send("u5", 4, grad_of(LO_Y3) + got(0), y=3)
        arrived("u6")
        image_send("u2", 5, grad_of(Y1) + got(1), y=1)

    def image_third():
        arrived("u4", "u5")
        image_send("ul", 6, grad_of(LO) + got(2) + got(4), lo=1)

    def image_out():
        arrived("u2", "u3", "ul")
        total = grad_of(OWN) + got(5) + got(3) + got(6)
        scale = s["scale_u"][...]
        unit = pic_ref[...].astype(F32) * scale
        gi_ref[...] = back_unit(unit, scale, total)

    send("l", img.at[slot(OWN)], img.at[slot(LO)], lo=1)
    z_first(0)
    send("y1", img.at[slot(OWN)], img.at[slot(Y1)], y=1)
    send("y3", img.at[slot(OWN)], img.at[slot(Y3)], y=3)
    send("t1", txt.at[slot(0)], txt.at[slot(1)], core=1)
    z_first(1)
    arrived("t1")
    for j in range(PARTS):
        s["bank"][j][4] = txt[pl.ds(rows + j * piece, piece), :]

    def image_lo():
        arrived("l")
        send("ly1", img.at[slot(LO)], img.at[slot(LO_Y1)], y=1)
        send("ly3", img.at[slot(LO)], img.at[slot(LO_Y3)], y=3)

    def image_y2():
        arrived("y1")
        send("y2", img.at[slot(Y1)], img.at[slot(Y2)], y=3)

    def image_lo_y2():
        arrived("ly3")
        send("ly2", img.at[slot(LO_Y3)], img.at[slot(LO_Y2)], y=1)

    z_second(0)
    z_first(2)
    image_lo()
    z_done(0)
    x_text(0)
    z_second(1)
    z_first(3)
    image_y2()
    x_second("g_", 0)
    z_done(1)
    x_text(1)
    text_in(0)
    z_second(2)
    image_lo_y2()
    x_second("g_", 1)
    z_done(2)
    x_text(2)
    text_in(1)
    z_second(3)
    arrived("y3", "ly1", "y2", "ly2")
    early()
    x_second("g_", 2)
    z_done(3)
    x_text(3)
    grads_out(0)
    arrived(*(f"t31_{j}" for j in range(PARTS)))
    early31()
    text_in(2)
    grads_x(0)
    x_second("g_", 3)
    grads_out(1)
    early_image()
    x_second("b_", 0)
    grads_x(1)
    grads_out(2)
    grads_z(0)
    text_in(3)
    grads_out(3)
    x_second("b_", 1)
    grads_x(2)
    image_first()
    grads_z_second(0)
    grads_x(3)
    x_second("b_", 2)
    grads_z(1)
    image_second()
    x_second("b_", 3)
    grads_z_second(1)
    grads_z(2)
    grads_z_second(2)
    grads_z(3)
    arrived("d1")
    text_out(0)
    image_third()
    grads_z_second(3)
    text_out(1)
    text_out(2)
    image_out()
    text_out(3)
    for copy in copies.values():
        copy.wait_send()


def local(picture_vectors, caption_vectors, logit_multiplier, logit_offset, partner_xor_codes):
    rows, wide = picture_vectors.shape
    in_vmem = pl.BlockSpec(memory_space=pltpu.VMEM)
    in_smem = pl.BlockSpec(memory_space=pltpu.SMEM)
    out = jax.ShapeDtypeStruct((rows, wide), F32)
    return pl.pallas_call(
        kernel,
        out_shape=(out, out),
        in_specs=[in_vmem, in_vmem, in_smem, in_smem, in_smem],
        out_specs=(in_vmem, in_vmem),
        scratch_shapes=[scratch(rows, wide)],
        compiler_params=pltpu.CompilerParams(
            collective_id=0, has_side_effects=True, vmem_limit_bytes=56 << 20
        ),
        name="contrastive_gradients",
    )(picture_vectors, caption_vectors, logit_multiplier, logit_offset, partner_xor_codes)


def solution(mesh):
    placed = (P(*WHOLE), P(*WHOLE), P(), P(), P())
    return jax.shard_map(
        local,
        mesh=mesh,
        in_specs=placed,
        out_specs=(P(*WHOLE), P(*WHOLE)),
        check_vma=False,
    )
```

time: 490 us -> 113 us (0.23)
  the two profiles are of different devices: /device:TPU:104 before, /device:TPU:1 now
where the time goes in v1:
time: 113 us
  Pallas kernels  108 us (96%)
  local copies, waits for them, and re-layouts  2.8 us (2%)
  between operations  1.94 us (2%)
    pallas_call x1, Pallas kernels, local(): pl.pallas_call(kernel, out_shape=(out, out), in_specs=[in_vmem, in_vmem,...  108 us
    unnamed x4, local copies, waits for them, and re-layouts  2.8 us

profile of v1, /device:TPU:1, one launch (start us, length us, event | category | flops | bytes accessed | tf_op | source)
XLA Modules:
  0.0 113.0 jit_solution(6309136238809359223)
XLA Ops:
  1.9 108.3 %contrastive_gradients.1 = (f32[128,1152]{1,0:T(8,128)}, f32[128,1152]{1,0:T(8,128)}) custom-call(bf16[128,1152]{1,0:T(8,128)(2,1)} %pic_ref.1, bf16[128,1152]{1,0:T(8,128)(2,1)} %cap_ref.1, f32[1]{0:T(128)S(6)} %copy.9.mult_ref, f32[1]{0:T(128)S(6)} %copy.10.off_ref, s32[4]{0:T(128)} %code_ref.1), custom_call_target="tpu_custom_call" | custom-call | tf_op jit(solution)/shard_map/contrastive_gradients/pallas_call | solution.py:479
  110.2 0.0 copy-start
  110.2 2.0 %copy.11 = f32[128,1152]{1,0:T(8,128)} copy(f32[128,1152]{1,0:T(8,128)} %get-tuple-element.4) | data formatting | bytes 1179648
  112.2 0.0 copy-done
  112.2 0.8 copy.12
Async XLA Ops:
  110.2 2.0 %copy-start = (f32[128,1152]{1,0:T(8,128)S(1)}, f32[128,1152]{1,0:T(8,128)}, u32[]{:S(2)}) copy-start(f32[128,1152]{1,0:T(8,128)} %get-tuple-element.5) | copy-start | bytes 1769476

commit v2 on v1

--- a/solution.py
+++ b/solution.py
@@ -119,7 +119,7 @@
     piece = rows // PARTS
     half = piece // 2
     img, txt, wgt = s["img"], s["txt"], s["wgt"]
-    copies = {}
+    copies, text_seen = {}, []
 
     def send(name, src, dst, **to):
         at = len(copies)
@@ -144,6 +144,9 @@
     def part(j):
         return pl.ds(j * piece, piece)
 
+    def text_at(j):
+        return 2 * rows + 3 * j * piece
+
     barrier = pltpu.get_barrier_semaphore()
     for to in PEERS:
         pl.semaphore_signal(barrier, inc=1, device_id=peer(**to), device_id_type=MESH)
@@ -181,9 +184,12 @@
         send(f"z2a_{j}", bank.at[1, near], bank.at[2, near], z=3)
         arrived(f"z3_{j}")
         send(f"z2b_{j}", bank.at[3, far], bank.at[2, far], z=1)
-        send(f"t31_{j}", bank.at[3], txt.at[pl.ds(2 * rows + j * piece, piece)], x=3, core=1)
         send(f"c1_{j}", bank.at[1], bank.at[5], core=1)
         send(f"c3_{j}", bank.at[3], bank.at[7], core=1)
+
+    def fetch_31(j):
+        bank = s["bank"][j]
+        send(f"t31_{j}", bank.at[3], txt.at[pl.ds(text_at(j), piece)], x=3, core=1)
 
     def z_done(j):
         bank = s["bank"][j]
@@ -229,28 +235,24 @@
         arrived(f"g_21_{j}", f"g_23_{j}")
         for m in range(2):
             near, far = x_done("g_", j, m)
-            base = 3 * rows + (2 * j + m) * piece
+            base = text_at(j) + (1 + m) * piece
             txt[pl.ds(base, half), :] = near
             txt[pl.ds(base + half, half), :] = far
 
-    def weigh(start, count, positive):
-        def tile(i, carry):
-            cols = pl.ds(pl.multiple_of(i * 2 * rows, 2 * rows), 2 * rows)
-            logits = lax.dot_general(
-                txt[pl.ds(start, count), :],
-                img[cols, :],
-                (((1,), (1,)), ((), ())),
-                preferred_element_type=F32,
-            )
-            factor = jax.nn.sigmoid(mult * logits + off)
-            if positive:
-                row = lax.broadcasted_iota(jnp.int32, factor.shape, 0)
-                col = lax.broadcasted_iota(jnp.int32, factor.shape, 1) + i * 2 * rows
-                factor = factor - jnp.where((row == col) & (row < rows), 1.0, 0.0)
-            wgt[pl.ds(start, count), cols] = (mult * factor).astype(BF)
-            return carry
-
-        lax.fori_loop(0, 4, tile, 0)
+    def weigh(start, count, at, wide_by, positive=False):
+        cols = pl.ds(at * rows, wide_by * rows)
+        logits = lax.dot_general(
+            txt[pl.ds(start, count), :],
+            img[cols, :],
+            (((1,), (1,)), ((), ())),
+            preferred_element_type=F32,
+        )
+        factor = jax.nn.sigmoid(mult * logits + off)
+        if positive:
+            row = lax.broadcasted_iota(jnp.int32, factor.shape, 0)
+            col = lax.broadcasted_iota(jnp.int32, factor.shape, 1)
+            factor = factor - jnp.where((row == col) & (row < rows), 1.0, 0.0)
+        wgt[pl.ds(start, count), cols] = (mult * factor).astype(BF)
 
     def text_grad(start, count):
         return jnp.dot(wgt[pl.ds(start, count), :], img[...], preferred_element_type=F32)
@@ -264,11 +266,18 @@
             preferred_element_type=F32,
         )
 
+    def weigh_in(j):
+        arrived(f"t31_{j}")
+        weigh(text_at(j), 3 * piece, 0, 8)
+
     def grads_out(j):
-        start = 3 * rows + 2 * j * piece
-        weigh(start, 2 * piece, False)
-        s["d_own"][j][...] = text_grad(start, 2 * piece).astype(BF)
+        grad = text_grad(text_at(j), 3 * piece).astype(BF)
+        s["d_own"][j][...] = grad[piece:]
         send(f"dc_{j}", s["d_own"][j], s["d_core"][j], core=1)
+        s["d31_out"][j][...] = grad[:piece]
+
+    def send_31(j):
+        send(f"d31_{j}", s["d31_out"][j], s["d31_in"][j], x=3, core=1)
 
     def grads_x(j):
         arrived(f"dc_{j}")
@@ -313,160 +322,209 @@
 
     def text_out(j):
         arrived(f"dz1_{j}", f"dz3_{j}")
+        if not text_seen:
+            text_seen.append(j)
+            arrived("d1")
         total = s["z_sum"][j][0] + s["z_r1"][j][...].astype(F32) + s["z_r3"][j][...].astype(F32)
         total = total + s["d_text"][part(j), :] + s["d_text_in"][part(j), :]
         scale = s["scale_v"][part(j), :]
         unit = cap_ref[part(j), :].astype(F32) * scale
         gt_ref[part(j), :] = back_unit(unit, scale, total)
 
-    def early():
-        weigh(0, 2 * rows, True)
+    def early(at):
+        weigh(0, 2 * rows, at, 2, at == OWN)
+        s["d_img"][pl.ds(at * rows, 2 * rows), :] = image_grad(0, 2 * rows, at)
+
+    def early_text():
         s["d_text"][...] = text_grad(0, 2 * rows)
         send("d1", s["d_text"].at[slot(1)], s["d_text_in"], core=1)
 
-    def early31():
-        weigh(2 * rows, rows, False)
-        grad = text_grad(2 * rows, rows).astype(BF)
-        for j in range(PARTS):
-            s["d31_out"][j][...] = grad[j * piece : (j + 1) * piece]
-            send(f"d31_{j}", s["d31_out"][j], s["d31_in"][j], x=3, core=1)
-
-    def early_image():
-        def tile(i, carry):
-            at = pl.ds(pl.multiple_of(i * 2 * rows, 2 * rows), 2 * rows)
-            s["d_img"][at, :] = lax.dot_general(
-                wgt[pl.ds(0, 3 * rows), at],
-                txt[pl.ds(0, 3 * rows), :],
-                (((0,), (0,)), ((), ())),
-                preferred_element_type=F32,
-            )
-            return carry
-
-        lax.fori_loop(0, 4, tile, 0)
-
     def late_image(at):
         here = pl.ds(at * rows, 2 * rows)
-        s["d_img"][here, :] = s["d_img"][here, :] + image_grad(3 * rows, 2 * rows, at)
-
-    def image_send(name, n, value, **to):
-        s["i_s"][n][...] = value.astype(BF)
-        send(name, s["i_s"][n], s["i_r"][n], **to)
-
-    def grad_of(at):
-        return s["d_img"][slot(at), :]
-
-    def got(n):
-        return s["i_r"][n][...].astype(F32)
+        s["d_img"][here, :] = s["d_img"][here, :] + image_grad(2 * rows, 3 * rows, at)
+
+    def half_send(name, n, at, adds, h, **to):
+        arrived(*(f"{add}_{h}" for add, _ in adds))
+        here = pl.ds(h * rows // 2, rows // 2)
+        value = s["d_img"][pl.ds(at * rows + h * rows // 2, rows // 2), :]
+        for _, m in adds:
+            value = value + s["i_r"][m][here, :].astype(F32)
+        s["i_s"][n][here, :] = value.astype(BF)
+        send(f"{name}_{h}", s["i_s"][n].at[here], s["i_r"][n].at[here], **to)
 
     def image_first():
         late_image(Y2)
-        image_send("u7", 0, grad_of(LO_Y2), y=1)
-        image_send("u6", 1, grad_of(Y2), y=3)
+        for h in range(2):
+            half_send("u7", 0, LO_Y2, [], h, y=1)
+            half_send("u6", 1, Y2, [], h, y=3)
+
+    def image_lo_y1():
         late_image(LO_Y1)
-        image_send("u4", 2, grad_of(LO_Y1), y=1)
-        late_image(Y1)
-        image_send("u3", 3, grad_of(Y3), y=3)
-        late_image(OWN)
-
-    def image_second():
-        arrived("u7")
-        image_send("u5", 4, grad_of(LO_Y3) + got(0), y=3)
-        arrived("u6")
-        image_send("u2", 5, grad_of(Y1) + got(1), y=1)
-
-    def image_third():
-        arrived("u4", "u5")
-        image_send("ul", 6, grad_of(LO) + got(2) + got(4), lo=1)
-
-    def image_out():
-        arrived("u2", "u3", "ul")
-        total = grad_of(OWN) + got(5) + got(3) + got(6)
-        scale = s["scale_u"][...]
-        unit = pic_ref[...].astype(F32) * scale
-        gi_ref[...] = back_unit(unit, scale, total)
-
-    send("l", img.at[slot(OWN)], img.at[slot(LO)], lo=1)
-    z_first(0)
-    send("y1", img.at[slot(OWN)], img.at[slot(Y1)], y=1)
-    send("y3", img.at[slot(OWN)], img.at[slot(Y3)], y=3)
-    send("t1", txt.at[slot(0)], txt.at[slot(1)], core=1)
-    z_first(1)
-    arrived("t1")
-    for j in range(PARTS):
-        s["bank"][j][4] = txt[pl.ds(rows + j * piece, piece), :]
-
-    def image_lo():
-        arrived("l")
-        send("ly1", img.at[slot(LO)], img.at[slot(LO_Y1)], y=1)
-        send("ly3", img.at[slot(LO)], img.at[slot(LO_Y3)], y=3)
-
-    def image_y2():
-        arrived("y1")
-        send("y2", img.at[slot(Y1)], img.at[slot(Y2)], y=3)
-
-    def image_lo_y2():
-        arrived("ly3")
-        send("ly2", img.at[slot(LO_Y3)], img.at[slot(LO_Y2)], y=1)
-
-    z_second(0)
-    z_first(2)
-    image_lo()
-    z_done(0)
-    x_text(0)
-    z_second(1)
-    z_first(3)
-    image_y2()
-    x_second("g_", 0)
-    z_done(1)
-    x_text(1)
-    text_in(0)
-    z_second(2)
-    image_lo_y2()
-    x_second("g_", 1)
-    z_done(2)
-    x_text(2)
-    text_in(1)
-    z_second(3)
-    arrived("y3", "ly1", "y2", "ly2")
-    early()
-    x_second("g_", 2)
-    z_done(3)
-    x_text(3)
-    grads_out(0)
-    arrived(*(f"t31_{j}" for j in range(PARTS)))
-    early31()
-    text_in(2)
-    grads_x(0)
-    x_second("g_", 3)
-    grads_out(1)
-    early_image()
-    x_second("b_", 0)
-    grads_x(1)
-    grads_out(2)
-    grads_z(0)
-    text_in(3)
-    grads_out(3)
-    x_second("b_", 1)
-    grads_x(2)
-    image_first()
-    grads_z_second(0)
-    grads_x(3)
-    x_second("b_", 2)
-    grads_z(1)
-    image_second()
-    x_second("b_", 3)
-    grads_z_second(1)
-    grads_z(2)
-    grads_z_second(2)
-    grads_z(3)
-    arrived("d1")
-    text_out(0)
-    image_third()
-    grads_z_second(3)
-    text_out(1)
-    text_out(2)
-    image_out()
-    text_out(3)
+        for h in range(2):
+            half_send("u4", 2, LO_Y1, [], h, y=1)
+
+    def image_u5(h):
+        half_send("u5", 4, LO_Y3, [("u7", 0)], h, y=3)
+
+    def image_u3(h):
+        half_send("u3", 3, Y3, [], h, y=3)
+
+    def image_u2(h):
+        half_send("u2", 5, Y1, [("u6", 1)], h, y=1)
+
+    def image_ul(h):
+        half_send("ul", 6, LO, [("u4", 2), ("u5", 4)], h, lo=1)
+
+    def image_out(h):
+        arrived(*(f"{name}_{h}" for name in ("u2", "u3", "ul")))
+        here = pl.ds(h * rows // 2, rows // 2)
+        total = s["d_img"][here, :]
+        for m in (5, 3, 6):
+            total = total + s["i_r"][m][here, :].astype(F32)
+        scale = s["scale_u"][here, :]
+        unit = pic_ref[here, :].astype(F32) * scale
+        gi_ref[here, :] = back_unit(unit, scale, total)
+
+    def pass_image(name, source, target, h, **to):
+        here = pl.ds(h * rows // 2, rows // 2)
+        at = lambda n: img.at[pl.ds(n * rows + h * rows // 2, rows // 2)]
+        send(f"{name}_{h}", at(source), at(target), **to)
+
+    def start():
+        pass_image("l", OWN, LO, 0, lo=1)
+        pass_image("l", OWN, LO, 1, lo=1)
+        for h in range(2):
+            pass_image("y1", OWN, Y1, h, y=1)
+            pass_image("y3", OWN, Y3, h, y=3)
+        send("t1", txt.at[slot(0)], txt.at[slot(1)], core=1)
+
+    def other_core():
+        arrived("t1")
+        for j in range(PARTS):
+            s["bank"][j][4] = txt[pl.ds(rows + j * piece, piece), :]
+
+    def img_lo(h):
+        arrived(f"l_{h}")
+        pass_image("ly3", LO, LO_Y3, h, y=3)
+        pass_image("ly1", LO, LO_Y1, h, y=1)
+
+    def img_y2(h):
+        arrived(f"y1_{h}")
+        pass_image("y2", Y1, Y2, h, y=3)
+
+    def img_lo_y2(h):
+        arrived(f"ly3_{h}")
+        pass_image("ly2", LO_Y3, LO_Y2, h, y=1)
+
+    def early_own():
+        early(OWN)
+
+    def early_y1():
+        arrived("y3_0", "y3_1")
+        early(Y1)
+
+    def early_lo():
+        arrived("ly1_0", "ly1_1")
+        early(LO_Y1)
+
+    def early_y2():
+        arrived("y2_0", "y2_1", "ly2_0", "ly2_1")
+        early(Y2)
+
+    steps = [
+        start,
+        (z_first, 0),
+        other_core,
+        (img_y2, 0),
+        (z_second, 0),
+        (fetch_31, 0),
+        (z_first, 2),
+        (img_lo, 0),
+        (img_y2, 1),
+        early_y1,
+        (z_first, 1),
+        (z_done, 0),
+        (x_text, 0),
+        (img_lo_y2, 0),
+        (z_second, 2),
+        (img_lo, 1),
+        early_own,
+        (x_second, "g_", 0),
+        (z_second, 1),
+        (fetch_31, 1),
+        (z_first, 3),
+        (z_done, 2),
+        (text_in, 0),
+        (img_lo_y2, 1),
+        early_lo,
+        (x_text, 2),
+        (fetch_31, 2),
+        (z_done, 1),
+        (x_text, 1),
+        (z_second, 3),
+        early_y2,
+        (weigh_in, 0),
+        (grads_out, 0),
+        (send_31, 0),
+        (x_second, "g_", 2),
+        early_text,
+        (z_done, 3),
+        (x_second, "g_", 1),
+        (grads_x, 0),
+        (x_text, 3),
+        (text_in, 2),
+        (weigh_in, 2),
+        (grads_out, 2),
+        (send_31, 2),
+        (text_in, 1),
+        (weigh_in, 1),
+        (grads_out, 1),
+        (x_second, "b_", 0),
+        (grads_x, 2),
+        (grads_x, 1),
+        (x_second, "g_", 3),
+        (fetch_31, 3),
+        (grads_z, 0),
+        (x_second, "b_", 2),
+        (grads_z_second, 0),
+        (x_second, "b_", 1),
+        (text_in, 3),
+        (send_31, 1),
+        (weigh_in, 3),
+        (grads_out, 3),
+        (send_31, 3),
+        image_first,
+        (grads_z, 2),
+        image_lo_y1,
+        (late_image, OWN),
+        (text_out, 0),
+        (late_image, Y1),
+        (grads_x, 3),
+        (grads_z, 1),
+        (grads_z_second, 2),
+        (image_u5, 0),
+        (image_u2, 0),
+        (x_second, "b_", 3),
+        (grads_z_second, 1),
+        (image_u5, 1),
+        (image_u3, 0),
+        (image_u3, 1),
+        (image_u2, 1),
+        (grads_z, 3),
+        (text_out, 2),
+        (image_ul, 0),
+        (text_out, 1),
+        (image_ul, 1),
+        (grads_z_second, 3),
+        (image_out, 0),
+        (text_out, 3),
+        (image_out, 1),
+    ]
+    for step in steps:
+        if isinstance(step, tuple):
+            step[0](*step[1:])
+        else:
+            step()
     for copy in copies.values():
         copy.wait_send()
 

time: 113 us -> 100 us (0.88)
  Pallas kernels: 108 us -> 95.5 us
    pallas_call x1, Pallas kernels: 108 us -> 95.5 us  [local(): pl.pallas_call(kernel, out_shape=(out, out), in_specs=[in_vmem, in_vmem,...]
where the time goes in v2:
time: 100 us
  Pallas kernels  95.5 us (96%)
  local copies, waits for them, and re-layouts  2.8 us (3%)
  between operations  1.94 us (2%)
    pallas_call x1, Pallas kernels, local(): pl.pallas_call(kernel, out_shape=(out, out), in_specs=[in_vmem, in_vmem,...  95.5 us
    unnamed x4, local copies, waits for them, and re-layouts  2.8 us

profile of v2, /device:TPU:1, one launch (start us, length us, event | category | flops | bytes accessed | tf_op | source)
XLA Modules:
  0.0 100.2 jit_solution(15353808337185723896)
XLA Ops:
  1.9 95.5 %contrastive_gradients.1 = (f32[128,1152]{1,0:T(8,128)}, f32[128,1152]{1,0:T(8,128)}) custom-call(bf16[128,1152]{1,0:T(8,128)(2,1)} %pic_ref.1, bf16[128,1152]{1,0:T(8,128)(2,1)} %cap_ref.1, f32[1]{0:T(128)S(6)} %copy.9.mult_ref, f32[1]{0:T(128)S(6)} %copy.10.off_ref, s32[4]{0:T(128)} %code_ref.1), custom_call_target="tpu_custom_call" | custom-call | tf_op jit(solution)/shard_map/contrastive_gradients/pallas_call | solution.py:537
  97.4 0.0 copy-start
  97.4 2.0 %copy.11 = f32[128,1152]{1,0:T(8,128)} copy(f32[128,1152]{1,0:T(8,128)} %get-tuple-element.4) | data formatting | bytes 1179648
  99.4 0.0 copy-done
  99.4 0.8 copy.12
Async XLA Ops:
  97.4 2.0 %copy-start = (f32[128,1152]{1,0:T(8,128)S(1)}, f32[128,1152]{1,0:T(8,128)}, u32[]{:S(2)}) copy-start(f32[128,1152]{1,0:T(8,128)} %get-tuple-element.5) | copy-start | bytes 1769476

commit v3 on v2

--- a/solution.py
+++ b/solution.py
@@ -107,6 +107,12 @@
         d_img=pltpu.VMEM((8 * rows, wide), F32),
         i_s=[unit] * 7,
         i_r=[unit] * 7,
+        pic=unit,
+        cap=unit,
+        mult=pltpu.SMEM((1,), F32),
+        off=pltpu.SMEM((1,), F32),
+        code=pltpu.SMEM((4,), jnp.int32),
+        load=pltpu.SemaphoreType.DMA((5,)),
         scale_u=pltpu.VMEM((rows, 1), F32),
         scale_v=pltpu.VMEM((rows, 1), F32),
         send=pltpu.SemaphoreType.DMA((160,)),
@@ -114,8 +120,10 @@
     )
 
 
-def kernel(pic_ref, cap_ref, mult_ref, off_ref, code_ref, gi_ref, gt_ref, s):
-    rows, wide = pic_ref.shape
+def kernel(pic_any, cap_any, mult_any, off_any, code_any, gi_ref, gt_ref, s):
+    rows, wide = pic_any.shape
+    pic_ref, cap_ref = s["pic"], s["cap"]
+    mult_ref, off_ref, code_ref = s["mult"], s["off"], s["code"]
     piece = rows // PARTS
     half = piece // 2
     img, txt, wgt = s["img"], s["txt"], s["wgt"]
@@ -151,6 +159,33 @@
     for to in PEERS:
         pl.semaphore_signal(barrier, inc=1, device_id=peer(**to), device_id_type=MESH)
 
+    loads = [
+        pltpu.make_async_copy(src, dst, s["load"].at[at])
+        for at, (src, dst) in enumerate(
+            (
+                (cap_any, cap_ref),
+                (pic_any, pic_ref),
+                (mult_any, mult_ref),
+                (off_any, off_ref),
+                (code_any, code_ref),
+            )
+        )
+    ]
+    for load in loads:
+        load.start()
+    loads[0].wait()
+    unit_v, scale_v = unit_rows(cap_ref[...])
+    s["scale_v"][...] = scale_v
+    own_text = unit_v.astype(BF)
+    txt[slot(0), :] = own_text
+    for j in range(PARTS):
+        s["bank"][j][0] = own_text[j * piece : (j + 1) * piece]
+    loads[1].wait()
+    unit_u, scale_u = unit_rows(pic_ref[...])
+    s["scale_u"][...] = scale_u
+    img[slot(OWN), :] = unit_u.astype(BF)
+    for load in loads[2:]:
+        load.wait()
     mult, off = mult_ref[0], off_ref[0]
     codes = [code_ref[i] for i in range(4)]
     code_a, code_b = jnp.int32(99), jnp.int32(-1)
@@ -160,16 +195,6 @@
     core_of = [code_a & 1, code_b & 1]
     z_of = [(code_a >> 1) & 3, (code_b >> 1) & 3]
     x_of = [(code_a >> 3) & 3, (code_b >> 3) & 3]
-
-    unit_v, scale_v = unit_rows(cap_ref[...])
-    s["scale_v"][...] = scale_v
-    own_text = unit_v.astype(BF)
-    txt[slot(0), :] = own_text
-    for j in range(PARTS):
-        s["bank"][j][0] = own_text[j * piece : (j + 1) * piece]
-    unit_u, scale_u = unit_rows(pic_ref[...])
-    s["scale_u"][...] = scale_u
-    img[slot(OWN), :] = unit_u.astype(BF)
     pl.semaphore_wait(barrier, len(PEERS))
 
     def z_first(j):
@@ -390,9 +415,10 @@
         at = lambda n: img.at[pl.ds(n * rows + h * rows // 2, rows // 2)]
         send(f"{name}_{h}", at(source), at(target), **to)
 
+    def start_lo(h):
+        pass_image("l", OWN, LO, h, lo=1)
+
     def start():
-        pass_image("l", OWN, LO, 0, lo=1)
-        pass_image("l", OWN, LO, 1, lo=1)
         for h in range(2):
             pass_image("y1", OWN, Y1, h, y=1)
             pass_image("y3", OWN, Y3, h, y=3)
@@ -433,90 +459,92 @@
 
     steps = [
         start,
+        (start_lo, 0),
         (z_first, 0),
+        (img_y2, 0),
+        (start_lo, 1),
         other_core,
-        (img_y2, 0),
         (z_second, 0),
+        (img_lo, 0),
+        (z_done, 0),
+        (z_first, 2),
+        (x_text, 0),
+        (img_lo, 1),
         (fetch_31, 0),
-        (z_first, 2),
-        (img_lo, 0),
         (img_y2, 1),
+        (z_first, 1),
         early_y1,
-        (z_first, 1),
-        (z_done, 0),
-        (x_text, 0),
+        (z_second, 2),
+        (x_second, "g_", 0),
+        (img_lo_y2, 1),
         (img_lo_y2, 0),
-        (z_second, 2),
-        (img_lo, 1),
+        (z_second, 1),
+        (z_done, 2),
+        (z_first, 3),
+        (fetch_31, 1),
+        (x_text, 2),
+        early_lo,
+        (z_done, 1),
         early_own,
-        (x_second, "g_", 0),
-        (z_second, 1),
-        (fetch_31, 1),
-        (z_first, 3),
-        (z_done, 2),
+        (fetch_31, 2),
         (text_in, 0),
-        (img_lo_y2, 1),
-        early_lo,
-        (x_text, 2),
-        (fetch_31, 2),
-        (z_done, 1),
         (x_text, 1),
-        (z_second, 3),
         early_y2,
+        (x_second, "g_", 2),
         (weigh_in, 0),
         (grads_out, 0),
+        (z_second, 3),
         (send_31, 0),
-        (x_second, "g_", 2),
-        early_text,
+        (x_second, "g_", 1),
         (z_done, 3),
-        (x_second, "g_", 1),
         (grads_x, 0),
+        (text_in, 2),
         (x_text, 3),
-        (text_in, 2),
         (weigh_in, 2),
+        (text_in, 1),
         (grads_out, 2),
-        (send_31, 2),
-        (text_in, 1),
+        (fetch_31, 3),
         (weigh_in, 1),
-        (grads_out, 1),
         (x_second, "b_", 0),
         (grads_x, 2),
+        (grads_out, 1),
+        early_text,
+        (x_second, "g_", 3),
         (grads_x, 1),
-        (x_second, "g_", 3),
-        (fetch_31, 3),
+        (x_second, "b_", 2),
         (grads_z, 0),
-        (x_second, "b_", 2),
+        (send_31, 2),
+        (text_in, 3),
+        (weigh_in, 3),
+        (send_31, 1),
+        image_first,
+        (grads_out, 3),
         (grads_z_second, 0),
         (x_second, "b_", 1),
-        (text_in, 3),
-        (send_31, 1),
-        (weigh_in, 3),
-        (grads_out, 3),
+        (grads_x, 3),
+        image_lo_y1,
+        (grads_z, 2),
+        (grads_z, 1),
+        (image_u5, 0),
+        (grads_z_second, 2),
+        (image_u5, 1),
         (send_31, 3),
-        image_first,
-        (grads_z, 2),
-        image_lo_y1,
+        (late_image, Y1),
+        (x_second, "b_", 3),
         (late_image, OWN),
-        (text_out, 0),
-        (late_image, Y1),
-        (grads_x, 3),
-        (grads_z, 1),
-        (grads_z_second, 2),
-        (image_u5, 0),
+        (grads_z_second, 1),
         (image_u2, 0),
-        (x_second, "b_", 3),
-        (grads_z_second, 1),
-        (image_u5, 1),
         (image_u3, 0),
+        (grads_z, 3),
         (image_u3, 1),
         (image_u2, 1),
-        (grads_z, 3),
-        (text_out, 2),
         (image_ul, 0),
-        (text_out, 1),
-        (image_ul, 1),
+        (text_out, 0),
         (grads_z_second, 3),
         (image_out, 0),
+        (image_ul, 1),
+        (text_out, 1),
+        (text_out, 2),
         (text_out, 3),
         (image_out, 1),
     ]
@@ -532,16 +560,16 @@
 def local(picture_vectors, caption_vectors, logit_multiplier, logit_offset, partner_xor_codes):
     rows, wide = picture_vectors.shape
     in_vmem = pl.BlockSpec(memory_space=pltpu.VMEM)
-    in_smem = pl.BlockSpec(memory_space=pltpu.SMEM)
+    anywhere = pl.BlockSpec(memory_space=pl.ANY)
     out = jax.ShapeDtypeStruct((rows, wide), F32)
     return pl.pallas_call(
         kernel,
         out_shape=(out, out),
-        in_specs=[in_vmem, in_vmem, in_smem, in_smem, in_smem],
+        in_specs=[anywhere] * 5,
         out_specs=(in_vmem, in_vmem),
         scratch_shapes=[scratch(rows, wide)],
         compiler_params=pltpu.CompilerParams(
-            collective_id=0, has_side_effects=True, vmem_limit_bytes=56 << 20
+            collective_id=0, has_side_effects=True, vmem_limit_bytes=38 << 20
         ),
         name="contrastive_gradients",
     )(picture_vectors, caption_vectors, logit_multiplier, logit_offset, partner_xor_codes)

time: 100 us -> 95.7 us (0.957); the launches traced: 100 us -> 94.8 us
  Pallas kernels: 95.5 us -> 89.2 us
    pallas_call x1, Pallas kernels: 95.5 us -> 89.2 us  [local(): pl.pallas_call(kernel, out_shape=(out, out), in_specs=[anywhere] * 5, out...]
    unnamed x4 -> x8, local copies, waits for them, and re-layouts: 2.8 us -> 3.55 us
where the time goes in v3:
time: 95.7 us; the launch traced here: 94.8 us
  Pallas kernels  89.2 us (93%)
  local copies, waits for them, and re-layouts  3.55 us (4%)
  between operations  1.97 us (2%)
    pallas_call x1, Pallas kernels, local(): pl.pallas_call(kernel, out_shape=(out, out), in_specs=[anywhere] * 5, out...  89.2 us
    unnamed x8, local copies, waits for them, and re-layouts  3.55 us

profile of v3, /device:TPU:1, one launch (start us, length us, event | category | flops | bytes accessed | tf_op | source)
XLA Modules:
  0.0 94.8 jit_solution(5034516317476264253)
XLA Ops:
  1.3 0.0 copy-start.2
  1.9 0.0 copy-done.2
  2.0 0.0 copy-start
  2.0 1.0 %copy-done = bf16[128,1152]{1,0:T(8,128)(2,1)S(1)} copy-done((bf16[128,1152]{1,0:T(8,128)(2,1)S(1)}, bf16[128,1152]{1,0:T(8,128)(2,1)}, u32[]{:S(2)}) %copy-start) | copy-done | bytes 294936
  2.9 0.0 copy-start.1
  2.9 1.0 %copy-done.1 = bf16[128,1152]{1,0:T(8,128)(2,1)S(1)} copy-done((bf16[128,1152]{1,0:T(8,128)(2,1)S(1)}, bf16[128,1152]{1,0:T(8,128)(2,1)}, u32[]{:S(2)}) %copy-start.1) | copy-done | bytes 294936
  3.9 89.2 %contrastive_gradients.1 = (f32[128,1152]{1,0:T(8,128)S(1)}, f32[128,1152]{1,0:T(8,128)S(1)}) custom-call(bf16[128,1152]{1,0:T(8,128)(2,1)S(1)} %copy-done, bf16[128,1152]{1,0:T(8,128)(2,1)S(1)} %copy-done.1, f32[1]{0:T(128)S(6)} %copy.9.mult_any, f32[1]{0:T(128)S(6)} %copy.10.off_any, s32[4]{0:T(128)S(1)} %copy-done.2), custom_call_target="tpu_custom_call" | custom-call | tf_op jit(solution)/shard_map/contrastive_gradients/pallas_call | solution.py:565
  93.1 0.8 copy.11
  93.9 0.8 copy.12
Async XLA Ops:
  1.3 0.7 copy-start.2
  2.0 1.0 %copy-start = (bf16[128,1152]{1,0:T(8,128)(2,1)S(1)}, bf16[128,1152]{1,0:T(8,128)(2,1)}, u32[]{:S(2)}) copy-start(bf16[128,1152]{1,0:T(8,128)(2,1)} %pic_any.1) | copy-start | bytes 884740
  2.9 1.0 %copy-start.1 = (bf16[128,1152]{1,0:T(8,128)(2,1)S(1)}, bf16[128,1152]{1,0:T(8,128)(2,1)}, u32[]{:S(2)}) copy-start(bf16[128,1152]{1,0:T(8,128)(2,1)} %cap_any.1) | copy-start | bytes 884740

commit v4 on v3

--- a/solution.py
+++ b/solution.py
@@ -1,3 +1,5 @@
+import functools
+
 import jax
 import jax.numpy as jnp
 from jax import lax
@@ -99,6 +101,7 @@
         d31_in=each(pltpu.VMEM((piece, wide), BF)),
         z_sum=each(pltpu.VMEM((4, piece, wide), F32)),
         z_s=each(pltpu.VMEM((3, piece, wide), BF)),
+        z_out=each(pltpu.VMEM((piece, wide), BF)),
         z_r2=each(pltpu.VMEM((piece, wide), BF)),
         z_r1=each(pltpu.VMEM((piece, wide), BF)),
         z_r3=each(pltpu.VMEM((piece, wide), BF)),
@@ -120,7 +123,7 @@
     )
 
 
-def kernel(pic_any, cap_any, mult_any, off_any, code_any, gi_ref, gt_ref, s):
+def kernel(lite, pic_any, cap_any, mult_any, off_any, code_any, gi_ref, gt_ref, s):
     rows, wide = pic_any.shape
     pic_ref, cap_ref = s["pic"], s["cap"]
     mult_ref, off_ref, code_ref = s["mult"], s["off"], s["code"]
@@ -195,15 +198,26 @@
     core_of = [code_a & 1, code_b & 1]
     z_of = [(code_a >> 1) & 3, (code_b >> 1) & 3]
     x_of = [(code_a >> 3) & 3, (code_b >> 3) & 3]
+    need_1 = (z_of[0] == 1) | (z_of[1] == 1)
+    slot_of = [jnp.where(z == 2, 1, z) for z in z_of] if lite else z_of
     pl.semaphore_wait(barrier, len(PEERS))
 
     def z_first(j):
         src = s["bank"][j].at[0]
+        if lite:
+            send(f"z3_{j}", src, s["bank"][j].at[3], z=3)
+            return
         send(f"z1_{j}", src, s["bank"][j].at[1], z=1)
         send(f"z3_{j}", src, s["bank"][j].at[3], z=3)
 
     def z_second(j):
         bank = s["bank"][j]
+        if lite:
+            arrived(f"z3_{j}")
+            s["z_out"][j][...] = jnp.where(need_1, bank[0], bank[3])
+            send(f"z1_{j}", s["z_out"][j], bank.at[1], z=1)
+            send(f"c3_{j}", bank.at[3], bank.at[7], core=1)
+            return
         near, far = pl.ds(0, half), pl.ds(half, half)
         arrived(f"z1_{j}")
         send(f"z2a_{j}", bank.at[1, near], bank.at[2, near], z=3)
@@ -218,6 +232,10 @@
 
     def z_done(j):
         bank = s["bank"][j]
+        if lite:
+            arrived(f"z1_{j}")
+            send(f"c1_{j}", bank.at[1], bank.at[5], core=1)
+            return
         arrived(f"z2a_{j}", f"z2b_{j}")
         send(f"c2_{j}", bank.at[2], bank.at[6], core=1)
 
@@ -248,10 +266,12 @@
 
     def x_text(j):
         bank = s["bank"][j]
-        arrived(f"c1_{j}", f"c2_{j}", f"c3_{j}")
+        arrived(f"c1_{j}", f"c3_{j}")
+        if not lite:
+            arrived(f"c2_{j}")
         for m in range(2):
             at = pl.ds(m * half, half)
-            picked = bank[core_of[m] * 4 + z_of[m]]
+            picked = bank[core_of[m] * 4 + slot_of[m]]
             s["g_near"][j][at, :] = picked[:half]
             s["g_far"][j][at, :] = picked[half:]
         x_send("g_", j, None, None)
@@ -322,12 +342,17 @@
         for h in range(2):
             at = pl.ds(h * half, half)
             a, b = got[0][h].astype(F32), got[1][h].astype(F32)
-            for k in range(4):
-                value = jnp.where(z_of[0] == k, a, zero) + jnp.where(z_of[1] == k, b, zero)
+            for k in (0, 1, 3) if lite else range(4):
+                to_k = [slot == k for slot in slot_of]
+                value = jnp.where(to_k[0], a, zero) + jnp.where(to_k[1], b, zero)
                 if k == 3:
                     value = value + s["d31_in"][j][at, :].astype(F32)
                 total[k, at, :] = value
         out = s["z_s"][j]
+        if lite:
+            out[1] = total[1].astype(BF)
+            send(f"dz1_{j}", out.at[1], s["z_r1"][j], z=1)
+            return
         out[0] = total[2].astype(BF)
         near, far = pl.ds(0, half), pl.ds(half, half)
         send(f"dz2a_{j}", out.at[0, near], s["z_r2"][j].at[near], z=3)
@@ -335,6 +360,14 @@
 
     def grads_z_second(j):
         total, out, got = s["z_sum"][j], s["z_s"][j], s["z_r2"][j]
+        if lite:
+            arrived(f"dz1_{j}")
+            came = s["z_r1"][j][...].astype(F32)
+            zero = jnp.zeros_like(came)
+            out[2] = (total[3] + jnp.where(need_1, zero, came)).astype(BF)
+            send(f"dz3_{j}", out.at[2], s["z_r3"][j], z=3)
+            total[0] = total[0] + jnp.where(need_1, came, zero)
+            return
         near, far = pl.ds(0, half), pl.ds(half, half)
         arrived(f"dz2a_{j}")
         out[1, far, :] = total[1, far, :].astype(BF)
@@ -346,11 +379,14 @@
         send(f"dz3_{j}", out.at[2], s["z_r3"][j], z=3)
 
     def text_out(j):
-        arrived(f"dz1_{j}", f"dz3_{j}")
+        arrived(f"dz3_{j}")
         if not text_seen:
             text_seen.append(j)
             arrived("d1")
-        total = s["z_sum"][j][0] + s["z_r1"][j][...].astype(F32) + s["z_r3"][j][...].astype(F32)
+        total = s["z_sum"][j][0] + s["z_r3"][j][...].astype(F32)
+        if not lite:
+            arrived(f"dz1_{j}")
+            total = total + s["z_r1"][j][...].astype(F32)
         total = total + s["d_text"][part(j), :] + s["d_text_in"][part(j), :]
         scale = s["scale_v"][part(j), :]
         unit = cap_ref[part(j), :].astype(F32) * scale
@@ -457,97 +493,190 @@
         arrived("y2_0", "y2_1", "ly2_0", "ly2_1")
         early(Y2)
 
-    steps = [
-        start,
-        (start_lo, 0),
-        (z_first, 0),
-        (img_y2, 0),
-        (start_lo, 1),
-        other_core,
-        (z_second, 0),
-        (img_lo, 0),
-        (z_done, 0),
-        (z_first, 2),
-        (x_text, 0),
-        (img_lo, 1),
-        (fetch_31, 0),
-        (img_y2, 1),
-        (z_first, 1),
-        early_y1,
-        (z_second, 2),
-        (x_second, "g_", 0),
-        (img_lo_y2, 1),
-        (img_lo_y2, 0),
-        (z_second, 1),
-        (z_done, 2),
-        (z_first, 3),
-        (fetch_31, 1),
-        (x_text, 2),
-        early_lo,
-        (z_done, 1),
-        early_own,
-        (fetch_31, 2),
-        (text_in, 0),
-        (x_text, 1),
-        early_y2,
-        (x_second, "g_", 2),
-        (weigh_in, 0),
-        (grads_out, 0),
-        (z_second, 3),
-        (send_31, 0),
-        (x_second, "g_", 1),
-        (z_done, 3),
-        (grads_x, 0),
-        (text_in, 2),
-        (x_text, 3),
-        (weigh_in, 2),
-        (text_in, 1),
-        (grads_out, 2),
-        (fetch_31, 3),
-        (weigh_in, 1),
-        (x_second, "b_", 0),
-        (grads_x, 2),
-        (grads_out, 1),
-        early_text,
-        (x_second, "g_", 3),
-        (grads_x, 1),
-        (x_second, "b_", 2),
-        (grads_z, 0),
-        (send_31, 2),
-        (text_in, 3),
-        (weigh_in, 3),
-        (send_31, 1),
-        image_first,
-        (grads_out, 3),
-        (grads_z_second, 0),
-        (x_second, "b_", 1),
-        (grads_x, 3),
-        image_lo_y1,
-        (grads_z, 2),
-        (grads_z, 1),
-        (image_u5, 0),
-        (grads_z_second, 2),
-        (image_u5, 1),
-        (send_31, 3),
-        (late_image, Y1),
-        (x_second, "b_", 3),
-        (late_image, OWN),
-        (grads_z_second, 1),
-        (image_u2, 0),
-        (image_u3, 0),
-        (grads_z, 3),
-        (image_u3, 1),
-        (image_u2, 1),
-        (image_ul, 0),
-        (text_out, 0),
-        (grads_z_second, 3),
-        (image_out, 0),
-        (image_ul, 1),
-        (text_out, 1),
-        (text_out, 2),
-        (text_out, 3),
-        (image_out, 1),
-    ]
+    if lite:
+        steps = [
+            start,
+            (z_first, 0),
+            (z_first, 1),
+            (start_lo, 0),
+            other_core,
+            (z_second, 0),
+            (fetch_31, 0),
+            (z_first, 2),
+            (start_lo, 1),
+            (img_lo, 0),
+            (z_second, 1),
+            (fetch_31, 1),
+            (img_y2, 0),
+            (z_done, 0),
+            (x_text, 0),
+            (z_second, 2),
+            (img_lo_y2, 0),
+            (z_done, 1),
+            (z_first, 3),
+            (img_lo, 1),
+            (img_y2, 1),
+            (x_text, 1),
+            (x_second, "g_", 0),
+            (z_done, 2),
+            (z_second, 3),
+            (x_second, "g_", 1),
+            (img_lo_y2, 1),
+            (x_text, 2),
+            early_own,
+            early_lo,
+            (text_in, 0),
+            (text_in, 1),
+            (fetch_31, 2),
+            early_y1,
+            (z_done, 3),
+            (x_second, "g_", 2),
+            early_y2,
+            (weigh_in, 0),
+            (x_text, 3),
+            (grads_out, 0),
+            (weigh_in, 1),
+            (fetch_31, 3),
+            (grads_out, 1),
+            (grads_x, 0),
+            (send_31, 0),
+            (x_second, "g_", 3),
+            (text_in, 2),
+            early_text,
+            (weigh_in, 2),
+            (grads_x, 1),
+            (x_second, "b_", 0),
+            (grads_out, 2),
+            (text_in, 3),
+            (weigh_in, 3),
+            image_first,
+            (send_31, 1),
+            (grads_out, 3),
+            (x_second, "b_", 1),
+            (grads_x, 2),
+            image_lo_y1,
+            (grads_z, 0),
+            (grads_z, 1),
+            (send_31, 2),
+            (x_second, "b_", 2),
+            (late_image, Y1),
+            (late_image, OWN),
+            (grads_z_second, 0),
+            (grads_x, 3),
+            (image_u5, 0),
+            (grads_z, 2),
+            (send_31, 3),
+            (grads_z_second, 1),
+            (image_u2, 1),
+            (x_second, "b_", 3),
+            (image_u2, 0),
+            (image_u5, 1),
+            (image_u3, 0),
+            (image_ul, 0),
+            (grads_z, 3),
+            (image_ul, 1),
+            (text_out, 0),
+            (grads_z_second, 2),
+            (image_u3, 1),
+            (image_out, 0),
+            (text_out, 1),
+            (grads_z_second, 3),
+            (text_out, 2),
+            (text_out, 3),
+            (image_out, 1),
+        ]
+    else:
+        steps = [
+            start,
+            (start_lo, 0),
+            (z_first, 0),
+            (img_y2, 0),
+            (start_lo, 1),
+            other_core,
+            (z_second, 0),
+            (img_lo, 0),
+            (z_done, 0),
+            (z_first, 2),
+            (x_text, 0),
+            (img_lo, 1),
+            (fetch_31, 0),
+            (img_y2, 1),
+            (z_first, 1),
+            early_y1,
+            (z_second, 2),
+            (x_second, "g_", 0),
+            (img_lo_y2, 1),
+            (img_lo_y2, 0),
+            (z_second, 1),
+            (z_done, 2),
+            (z_first, 3),
+            (fetch_31, 1),
+            (x_text, 2),
+            early_lo,
+            (z_done, 1),
+            early_own,
+            (fetch_31, 2),
+            (text_in, 0),
+            (x_text, 1),
+            early_y2,
+            (x_second, "g_", 2),
+            (weigh_in, 0),
+            (grads_out, 0),
+            (z_second, 3),
+            (send_31, 0),
+            (x_second, "g_", 1),
+            (z_done, 3),
+            (grads_x, 0),
+            (text_in, 2),
+            (x_text, 3),
+            (weigh_in, 2),
+            (text_in, 1),
+            (grads_out, 2),
+            (fetch_31, 3),
+            (weigh_in, 1),
+            (x_second, "b_", 0),
+            (grads_x, 2),
+            (grads_out, 1),
+            early_text,
+            (x_second, "g_", 3),
+            (grads_x, 1),
+            (x_second, "b_", 2),
+            (grads_z, 0),
+            (send_31, 2),
+            (text_in, 3),
+            (weigh_in, 3),
+            (send_31, 1),
+            image_first,
+            (grads_out, 3),
+            (grads_z_second, 0),
+            (x_second, "b_", 1),
+            (grads_x, 3),
+            image_lo_y1,
+            (grads_z, 2),
+            (grads_z, 1),
+            (image_u5, 0),
+            (grads_z_second, 2),
+            (image_u5, 1),
+            (send_31, 3),
+            (late_image, Y1),
+            (x_second, "b_", 3),
+            (late_image, OWN),
+            (grads_z_second, 1),
+            (image_u2, 0),
+            (image_u3, 0),
+            (grads_z, 3),
+            (image_u3, 1),
+            (image_u2, 1),
+            (image_ul, 0),
+            (text_out, 0),
+            (grads_z_second, 3),
+            (image_out, 0),
+            (image_ul, 1),
+            (text_out, 1),
+            (text_out, 2),
+            (text_out, 3),
+            (image_out, 1),
+        ]
     for step in steps:
         if isinstance(step, tuple):
             step[0](*step[1:])
@@ -557,22 +686,28 @@
         copy.wait_send()
 
 
-def local(picture_vectors, caption_vectors, logit_multiplier, logit_offset, partner_xor_codes):
-    rows, wide = picture_vectors.shape
+def call(lite, *args):
+    rows, wide = args[0].shape
     in_vmem = pl.BlockSpec(memory_space=pltpu.VMEM)
     anywhere = pl.BlockSpec(memory_space=pl.ANY)
     out = jax.ShapeDtypeStruct((rows, wide), F32)
     return pl.pallas_call(
-        kernel,
+        functools.partial(kernel, lite),
         out_shape=(out, out),
         in_specs=[anywhere] * 5,
         out_specs=(in_vmem, in_vmem),
         scratch_shapes=[scratch(rows, wide)],
         compiler_params=pltpu.CompilerParams(
-            collective_id=0, has_side_effects=True, vmem_limit_bytes=38 << 20
+            collective_id=0 if lite else 1, has_side_effects=True, vmem_limit_bytes=38 << 20
         ),
-        name="contrastive_gradients",
-    )(picture_vectors, caption_vectors, logit_multiplier, logit_offset, partner_xor_codes)
+        name="contrastive_lite" if lite else "contrastive_full",
+    )(*args)
+
+
+def local(*args):
+    z_codes = (args[4] >> 1) & 3
+    both = jnp.any(z_codes == 1) & jnp.any(z_codes == 2)
+    return lax.cond(both, functools.partial(call, False), functools.partial(call, True), *args)
 
 
 def solution(mesh):

time: 95.7 us -> 87.4 us (0.913)
  Pallas kernels: 89.2 us -> 81.5 us
  local copies, waits for them, and re-layouts: 3.55 us -> 2.28 us
    pallas_call x1, Pallas kernels: 89.2 us -> 81.5 us  [call(): pl.pallas_call(functools.partial(kernel, lite), out_shape=(out, out), in_...]
    unnamed x8 -> x4, local copies, waits for them, and re-layouts: 3.55 us -> 2.28 us
where the time goes in v4:
time: 87.4 us; the launch traced here: 86.5 us
  Pallas kernels  81.5 us (93%)
  local copies, waits for them, and re-layouts  2.28 us (3%)
  between operations  1.95 us (2%)
    pallas_call x1, Pallas kernels, call(): pl.pallas_call(functools.partial(kernel, lite), out_shape=(out, out), in_...  81.5 us
    unnamed x4, local copies, waits for them, and re-layouts  2.28 us

profile of v4, /device:TPU:1, one launch (start us, length us, event | category | flops | bytes accessed | tf_op | source)
XLA Modules:
  0.0 86.5 jit_solution(6956815058370055009)
XLA Ops:
  0.6 0.0 copy-start
  0.6 0.6 copy-done
  1.3 0.6 compare_reduce_fusion
  3.2 81.7 %conditional.1 = ((f32[128,1152]{1,0:T(8,128)S(1)}, f32[128,1152]{1,0:T(8,128)S(1)})) conditional(s32[]{:T(128)} %convert_element_type.3, (bf16[128,1152]{1,0:T(8,128)(2,1)}, bf16[128,1152]{1,0:T(8,128)(2,1)}, f32[1]{0:T(128)}, f32[1]{0:T(128)}, s32[4]{0:T(128)S(1)}) %tuple.25, (bf16[128,1152]{1,0:T(8,128)(2,1)}, bf16[128,1152]{1,0:T(8,128)(2,1)}, ...), branch_computations={%region_2.0_spmd, %region_3.0_spmd} | conditional | bytes 8 | solution.py:710
  3.2 81.5 %contrastive_lite.1 = (f32[128,1152]{1,0:T(8,128)S(1)}, f32[128,1152]{1,0:T(8,128)S(1)}) custom-call(bf16[128,1152]{1,0:T(8,128)(2,1)} %get-tuple-element.46.pic_any, bf16[128,1152]{1,0:T(8,128)(2,1)} %get-tuple-element.48.cap_any, f32[1]{0:T(128)} %get-tuple-element.50.mult_any, f32[1]{0:T(128)} %get-tuple-element.52.off_any, s32[4]{0:T(128)S(1)} %get-tuple-element.24.code_any), custom_call_target="tpu_custom_call" | custom-call | tf_op jit(solution)/shard_map/cond/branch_0_fun/contrastive_lite/pallas_call | solution.py:694
  84.9 0.8 copy.25
  85.7 0.8 copy.26
Async XLA Ops:
  0.6 0.7 copy-start

commit v5 on v4

--- a/solution.py
+++ b/solution.py
@@ -706,7 +706,8 @@
 
 def local(*args):
     z_codes = (args[4] >> 1) & 3
-    both = jnp.any(z_codes == 1) & jnp.any(z_codes == 2)
+    asked = jnp.where(z_codes == 1, 1, jnp.where(z_codes == 2, 2, 0))
+    both = lax.reduce(asked, jnp.int32(0), lax.bitwise_or, (0,)) == 3
     return lax.cond(both, functools.partial(call, False), functools.partial(call, True), *args)
 
 

time: 87.4 us -> 87.4 us (level)
    another operation x0 -> x1, other arithmetic: none -> 1.3 us  [local(): both = lax.reduce(asked, jnp.int32(0), lax.bitwise_or, (0,)) == 3]
where the time goes in v5:
time: 87.4 us; the launch traced here: 86.5 us
  Pallas kernels  81.5 us (93%)
  local copies, waits for them, and re-layouts  2.28 us (3%)
  other arithmetic  1.3 us (1%)
  between operations  1.3 us (1%)
    pallas_call x1, Pallas kernels, call(): pl.pallas_call(functools.partial(kernel, lite), out_shape=(out, out), in_...  81.5 us
    unnamed x4, local copies, waits for them, and re-layouts  2.28 us

profile of v5, /device:TPU:1, one launch (start us, length us, event | category | flops | bytes accessed | tf_op | source)
XLA Modules:
  0.0 86.5 jit_solution(10186023067878837636)
XLA Ops:
  0.6 1.3 %fusion = s32[]{:T(128)} fusion(s32[4]{0:T(128)} %param.11), kind=kLoop, calls=%fused_computation.2 | loop fusion | flops 27 | bytes 20 | tf_op jit(solution)/shard_map/reduce | solution.py:710
  2.6 0.0 copy-start
  2.6 0.6 copy-done
  3.2 81.7 %conditional.1 = ((f32[128,1152]{1,0:T(8,128)S(1)}, f32[128,1152]{1,0:T(8,128)S(1)})) conditional(s32[]{:T(128)} %convert_element_type.3, (bf16[128,1152]{1,0:T(8,128)(2,1)}, bf16[128,1152]{1,0:T(8,128)(2,1)}, f32[1]{0:T(128)}, f32[1]{0:T(128)}, s32[4]{0:T(128)S(1)}) %tuple.24, (bf16[128,1152]{1,0:T(8,128)(2,1)}, bf16[128,1152]{1,0:T(8,128)(2,1)}, ...), branch_computations={%region_1.2_spmd, %region_2.3_spmd} | conditional | bytes 8 | solution.py:711
  3.2 81.5 %contrastive_lite.1 = (f32[128,1152]{1,0:T(8,128)S(1)}, f32[128,1152]{1,0:T(8,128)S(1)}) custom-call(bf16[128,1152]{1,0:T(8,128)(2,1)} %get-tuple-element.46.pic_any, bf16[128,1152]{1,0:T(8,128)(2,1)} %get-tuple-element.48.cap_any, f32[1]{0:T(128)} %get-tuple-element.50.mult_any, f32[1]{0:T(128)} %get-tuple-element.52.off_any, s32[4]{0:T(128)S(1)} %get-tuple-element.24.code_any), custom_call_target="tpu_custom_call" | custom-call | tf_op jit(solution)/shard_map/cond/branch_0_fun/contrastive_lite/pallas_call | solution.py:694
  84.9 0.8 copy.25
  85.7 0.8 copy.26
Async XLA Ops:
  2.6 0.7 copy-start
